TPU v7x, 32 devices: a whole 2x2x4 slice. The times are simulated.
32 devices in a mesh: seq: 8 (over z, y), blk: 4 (over x, core).
Axes of the slice: x: 2, y: 2, z: 4, core: 2. Of those that a mesh axis runs over, the one named last changes fastest.
Arguments:
- chars: bfloat16 [32, 2048, 512], P('seq', 'blk'), may hold values from -6 to 6
- seg_lengths: int32 [32, 512], P('seq'), may hold values from 1 to 16, as said below
- memory: bfloat16 [32, 512, 512], P('seq', 'blk'), may hold values from -6 to 6
- grad_out: bfloat16 [32, 2048, 512], P('seq', 'blk'), may hold values from -6 to 6
- w_query: bfloat16 [512, 512], replicated, may hold values from -0.25 to 0.25
- w_key: bfloat16 [512, 512], replicated, may hold values from -0.25 to 0.25
- w_value: bfloat16 [512, 512], replicated, may hold values from -0.25 to 0.25
- w_rel: bfloat16 [512, 512], replicated, may hold values from -0.375 to 0.375
- w_out: bfloat16 [512, 512], replicated, may hold values from -1 to 1
- w_up: bfloat16 [512, 2048], replicated, may hold values from -0.25 to 0.25
- w_down: bfloat16 [2048, 512], replicated, may hold values from -0.125 to 0.125
- bias_u: bfloat16 [8, 64], replicated, may hold values from -3 to 3
- bias_v: bfloat16 [8, 64], replicated, may hold values from -3 to 3
- gain_one: bfloat16 [512], replicated, may hold values from 0.5 to 1.5
- shift_one: bfloat16 [512], replicated, may hold values from -2 to 2
- gain_two: bfloat16 [512], replicated, may hold values from 0.5 to 1.5
- shift_two: bfloat16 [512], replicated, may hold values from -2 to 2
- bias_up: bfloat16 [2048], replicated, may hold values from -2 to 2
- bias_down: bfloat16 [512], replicated, may hold values from -2 to 2
Outputs:
- out_chars: bfloat16 [32, 2048, 512], P('seq', 'blk')
- grad_chars: float32 [32, 2048, 512], P('seq', 'blk')
- new_memory: bfloat16 [32, 512, 512], P('seq', 'blk')
- grad_w_query: float32 [512, 512], replicated
- grad_w_key: float32 [512, 512], replicated
- grad_w_value: float32 [512, 512], replicated
- grad_w_rel: float32 [512, 512], replicated
- grad_w_out: float32 [512, 512], replicated
- grad_w_up: float32 [512, 2048], replicated
- grad_w_down: float32 [2048, 512], replicated
- grad_bias_u: float32 [8, 64], replicated
- grad_bias_v: float32 [8, 64], replicated
- grad_gain_one: float32 [512], replicated
- grad_shift_one: float32 [512], replicated
- grad_gain_two: float32 [512], replicated
- grad_shift_two: float32 [512], replicated
- grad_bias_up: float32 [2048], replicated
- grad_bias_down: float32 [512], replicated
Inputs may be any that keep to these rules, and one draw needn't show every extreme that they name: `seg_lengths`: each row lists the lengths of the 512 segments of one sequence in order; they sum to 2048 and the longest is 16; the first 384 segments of every sequence are one byte long.
All inputs are finite; a program needn't handle non-finite values.
Results may differ from a plain program's by a relative error of at most 0.015.
Values may be sent and summed in bfloat16 or wider, within the bound.
A program may use at most 192 MiB of HBM per device.

v0:
```python
import functools
import math
import types

import jax
import jax.numpy as jnp
import numpy as np
from jax import lax
from jax.experimental import pallas as pl
from jax.experimental.pallas import tpu as pltpu
from jax.sharding import PartitionSpec as P

F32, BF16 = jnp.float32, jnp.bfloat16
NT = (((1,), (1,)), ((), ()))


def mm(a, b):
    return jnp.dot(a, b, preferred_element_type=F32)


def mm_nt(a, b):
    return lax.dot_general(a, b, NT, preferred_element_type=F32)


def normalize(value):
    center = value - jnp.mean(value, axis=-1, keepdims=True)
    inv = lax.rsqrt(jnp.mean(center * center, axis=-1, keepdims=True) + 1e-05)
    return center * inv, inv


def norm_back(grad, unit, inv, gain):
    scaled = grad * gain
    along = jnp.mean(scaled * unit, axis=-1, keepdims=True)
    return inv * (scaled - jnp.mean(scaled, axis=-1, keepdims=True) - unit * along)


def gelu_parts(value):
    gate = 0.5 + 0.5 * lax.erf(value * 0.7071067811865476)
    return gate, gate + value * jnp.exp(-0.5 * value * value) * 0.3989422804014327


def ramp(shape, dim):
    return lax.broadcasted_iota(jnp.int32, shape, dim)


MESH = pl.DeviceIdType.MESH
HALF = 256
STEPS = 11
AXES = ("x", "y", "near", "far")
PIECES = tuple((1024, f"tile{n}") for n in range(4)) + ((512, "middle"),) + tuple((512, f"pair{n}") for n in range(4))
BASES = tuple(sum(rows for rows, unused in PIECES[:n]) for n in range(len(PIECES) + 1))
VECTORS = ("bias_u", "bias_v", "gain_one", "shift_one", "gain_two", "shift_two", "bias_up", "bias_down")
ORDERS = (
    (("y", "x", "near", "far"), ("x", "near", "y", "far")),
    (("near", "y", "far", "x"), ("x", "y", "near", "far")),
    (("near", "far", "y", "x"), ("y", "x", "near", "far")),
    (("far", "y", "x", "near"), ("y", "x", "near", "far")),
    (("y", "near", "x", "far"), ("x", "y", "far", "near")),
    (("y", "x", "near", "far"), ("y", "near", "x", "far")),
    (("near", "x", "y", "far"), ("x", "far", "y", "near")),
    (("y", "x", "near", "far"), ("near", "y", "x", "far")),
    (("y", "near", "x", "far"), ("near", "x", "y", "far")),
)
DURING = (
    ((0, 0),), ((1, 0),), ((2, 0),), ((0, 1), (3, 0)), ((1, 1),), ((2, 1), (3, 1), (4, 0)), ((0, 2),), (),
    (), ((1, 2), (4, 1)), ((5, 0),), (), ((2, 2),), (), ((5, 1),), ((6, 0),), ((0, 3), (3, 2)), (),
    ((1, 3), (6, 1)), ((4, 2),), ((7, 0), (2, 3)), (), ((5, 2),), ((0, 4), (7, 1)), ((1, 4), (3, 3)),
    ((8, 0), (4, 3), (6, 2)), ((2, 4),),
)
AFTER = (
    (8, 1), (0, 5), (7, 2), (5, 3), (1, 5), (3, 4), (4, 4), (6, 3), (2, 5), (8, 2), (7, 3), (5, 4), (0, 6),
    (1, 6), (6, 4), (3, 5), (4, 5), (8, 3), (2, 6), (0, 7), (7, 4), (5, 5), (8, 4), (1, 7), (6, 5), (3, 6),
    (4, 6), (2, 7), (0, 8), (7, 5), (5, 6), (8, 5), (6, 6), (3, 7), (1, 8), (4, 7), (2, 8), (7, 6), (0, 9),
    (6, 7), (5, 7), (8, 6), (3, 8), (4, 8), (0, 10), (1, 9), (2, 9), (7, 7), (8, 7), (5, 8), (1, 10), (6, 8),
    (2, 10), (4, 9), (7, 8), (3, 9), (8, 8), (4, 10), (5, 9), (6, 9), (3, 10), (7, 9), (5, 10), (8, 9),
    (6, 10), (7, 10), (8, 10),
)
BACK_DURING = (6, 8, 11, 13, 16, 21, 22, 24)
BACK_AFTER = (10, 14, 20, 45, 49, 55, 56, 61)


class Place:
    def __init__(self):
        self.s = lax.axis_index("seq")
        self.b = lax.axis_index("blk")
        self.z, self.y = self.s // 2, self.s % 2
        self.x, self.c = self.b // 2, self.b % 2
        self.bit = dict(x=self.x, y=self.y, near=self.z % 2, far=self.z // 2)

    def group(self, k):
        return (self.s, (self.b + k) % 4)

    def core(self):
        return (self.s, self.b + 1 - 2 * self.c)

    def across(self):
        return (self.s, self.b + 2 - 4 * self.x)

    def move(self, axis):
        reach = dict(x=(0, 2), y=(1, 0), near=(2, 0), far=(4, 0))[axis]
        turn = 1 - 2 * self.bit[axis]
        return reach[0] * turn, reach[1] * turn

    def step(self, zero, one):
        if zero == one:
            return self.pair(zero), self.bit[zero]
        away = [self.move(zero)[m] * (1 - self.c) + self.move(one)[m] * self.c for m in (0, 1)]
        bit = self.bit[zero] * (1 - self.c) + self.bit[one] * self.c
        return (self.s + away[0], self.b + away[1]), bit

    def pair(self, axis):
        away = self.move(axis)
        return (self.s + away[0], self.b + away[1])


def rows_at(start, size):
    return pl.ds(pl.multiple_of(start, 16), size)


def remote(src, dst, send, recv, to):
    return pltpu.make_async_remote_copy(src, dst, send, recv, device_id=to, device_id_type=MESH)


class Sum:
    def __init__(self, place, total, land, out, send, recv, store):
        self.p, self.g, self.land, self.out = place, total, land, out
        self.send, self.recv, self.store = send, recv, store
        self.steps = [[place.step(*axes) for axes in zip(*orders)] for orders in ORDERS]

    def offset(self, k, n):
        start = BASES[k] + self.p.c * (PIECES[k][0] // 2)
        for m in range(n):
            start = start + self.steps[k][m][1] * (PIECES[k][0] >> (m + 2))
        return start

    def lands(self, k, n, start=0, size=None):
        rows = PIECES[k][0] >> (n + 1)
        return self.land[n].at[rows_at((BASES[k] >> (n + 1)) + start, rows if size is None else size)]

    def copies(self, step, k, landing=False):
        p, g = self.p, self.g
        rows = PIECES[k][0]

        def copy(src, dst, to):
            return remote(src, dst, self.send.at[k], self.recv.at[k, step], to)

        if step == 0:
            half = rows // 2
            return copy(g.at[rows_at(BASES[k] + (1 - p.c) * half, half)], self.lands(k, 0), p.core())
        if step <= 4:
            to, bit = self.steps[k][step - 1]
            size = rows >> (step + 1)
            away = self.offset(k, step - 1) + (1 - bit) * size
            return copy(g.at[rows_at(away, size)], self.lands(k, step), to)
        if step <= 8:
            n = 8 - step
            to, bit = self.steps[k][n]
            size = rows >> (n + 2)
            dst = self.lands(k, n, (1 - bit if landing else bit) * size, size)
            src = self.lands(k, 3, bit * size, size) if n == 3 else self.lands(k, n + 1)
            return copy(src, dst, to)
        half = rows // 2
        span = BASES[k] + (1 - p.c if landing else p.c) * half
        return copy(self.lands(k, 0), self.out.at[rows_at(span, half)], p.core())

    def own(self, k):
        half = PIECES[k][0] // 2
        span = rows_at(BASES[k] + self.p.c * half, half)
        return pltpu.make_async_copy(self.lands(k, 0), self.out.at[span], self.store.at[k])

    def add(self, k, n, start, size):
        span = rows_at(self.offset(k, n) + start, size)
        self.g[span] = (self.g[span].astype(F32) + self.lands(k, n, start, size)[...].astype(F32)).astype(BF16)

    def step(self, k, step):
        g = self.g
        rows = PIECES[k][0]
        if step > 0:
            self.copies(step - 1, k).wait_send()
            self.copies(step - 1, k, landing=True).wait_recv()
        if 1 <= step <= 4:
            half = rows >> (step + 1)
            bit = self.steps[k][step - 1][1]
            self.add(k, step - 1, (1 - bit) * half, half)
            self.copies(step, k).start()
            self.add(k, step - 1, bit * half, half)
        elif step == 5:
            size = rows >> 5
            total = g[rows_at(self.offset(k, 4), size)].astype(F32) + self.lands(k, 4)[...].astype(F32)
            self.lands(k, 3, self.steps[k][3][1] * size, size)[...] = total.astype(BF16)
            self.copies(step, k).start()
        elif step < STEPS - 1:
            self.copies(step, k).start()
        if 6 <= step <= 8:
            n = 8 - step
            size = rows >> (n + 2)
            self.lands(k, n, self.steps[k][n][1] * size, size)[...] = self.lands(k, n + 1)[...]
        if step == STEPS - 2:
            self.own(k).start()
        if step == STEPS - 1:
            self.own(k).wait()


def pair_lanes(p, start=0, size=128):
    if isinstance(p, int):
        return slice(p * 128 + start, p * 128 + start + size)
    return pl.ds(pl.multiple_of(p * 128 + start, size), size)


def lane_mask(par):
    lane = ramp((1, 128), 1)
    return jnp.where((lane >= 64) == bool(par), 1.0, 0.0).astype(BF16)


def flip_matrix():
    return jnp.where(ramp((HALF, HALF), 0) + ramp((HALF, HALF), 1) == HALF - 1, 1.0, 0.0).astype(BF16)


def flip(flip_low, value):
    return jnp.concatenate(
        [mm(flip_low, value[r : r + HALF]) for r in range(0, value.shape[0], HALF)], axis=0
    ).astype(value.dtype)


def pool_matrix(end, length, first_place, places):
    place = (ramp((end.shape[0], places), 1) + first_place).astype(F32)
    return jnp.where((place < end) & (place >= end - length), 1.0, 0.0).astype(BF16)


def query_block(n, seg):
    keys = seg + HALF * (n + 1)
    return slice(n * HALF, (n + 1) * HALF), keys, 2 * seg - keys


def attend(n, seg, r):
    seen = ramp((HALF, HALF), 1) <= ramp((HALF, HALF), 0)
    lane = ramp((HALF, 128), 1)
    rows, keys, skip = query_block(n, seg)

    def products(head):
        lanes, keep = pair_lanes(head // 2), lane_mask(head % 2)
        near = mm_nt(r.query_u[rows, lanes] * keep, r.key[0:keys, lanes])
        return near, mm_nt(r.query_v[rows, lanes] * keep, r.place[skip : 2 * seg, lanes])

    ahead = products(0)
    for p in range(4):
        mixed, scale = [], []
        for head in (2 * p, 2 * p + 1):
            near, far = ahead
            ahead = products(head + 1) if head < 7 else None
            scores = near + pltpu.roll(far, keys - (HALF - 1), 1, stride=1, stride_axis=0)
            scores = jnp.concatenate(
                [scores[:, : keys - HALF], jnp.where(seen, scores[:, keys - HALF :], -1e30)], axis=1
            )
            expo = jnp.exp(scores - jnp.max(scores, axis=1, keepdims=True))
            probs = expo.astype(BF16)
            r.probs[head, rows, 0:keys] = probs
            mixed.append(mm(probs, r.value[0:keys, pair_lanes(p)]))
            scale.append(1.0 / jnp.sum(expo, axis=1, keepdims=True))
        scale = jnp.where(lane >= 64, scale[1], scale[0])
        r.scale[rows, pair_lanes(p)] = scale
        r.mixed[rows, pair_lanes(p)] = (jnp.where(lane >= 64, mixed[1], mixed[0]) * scale).astype(BF16)


def attend_back_pair(p, seg, r, between):
    lanes = pair_lanes(p)
    flip_low = flip_matrix()
    scale = 0.125
    lane = ramp((HALF, 128), 1)
    sums = [None] * 6
    bias = []
    for n in range(seg // HALF):
        rows, keys, skip = query_block(n, seg)
        key, value, place = r.key[0:keys, lanes], r.value[0:keys, lanes], r.place[skip : 2 * seg, lanes]
        grad_u, grad_v = [], []
        for par in range(2):
            keep = lane_mask(par)
            feats = pair_lanes(p, par * 64, 64)
            probs = r.probs[2 * p + par, rows, 0:keys]
            turned = mm(flip_low, probs)
            grad_mixed = r.grad_mixed[rows, lanes] * keep
            delta = jnp.sum(grad_mixed.astype(F32) * r.mixed_flip[rows, lanes].astype(F32), axis=1, keepdims=True)
            grad_scores = turned * (mm_nt(grad_mixed, value) - delta)
            near = grad_scores.astype(BF16)
            far = pltpu.roll(grad_scores, 0, 1, stride=1, stride_axis=0).astype(BF16)
            grad_u.append(mm(near, key) * scale)
            grad_v.append(mm(far, place) * scale)
            now = (
                mm(r.query_u_t[feats, rows], near),
                mm(r.grad_mixed_t[feats, rows], probs),
                mm(r.query_v_t[feats, rows], far),
            )
            for m in range(3):
                slot = par * 3 + m
                if n == 0:
                    sums[slot] = now[m]
                else:
                    old, new = sums[slot], now[m]
                    cut = old.shape[1]
                    if m < 2:
                        sums[slot] = jnp.concatenate([new[:, :cut] + old, new[:, cut:]], axis=1)
                    else:
                        sums[slot] = jnp.concatenate([new[:, :-cut], new[:, -cut:] + old], axis=1)
            between(n * 2 + par)
        grad_u = jnp.where(lane >= 64, grad_u[1], grad_u[0])
        grad_v = jnp.where(lane >= 64, grad_v[1], grad_v[0])
        bias.append((jnp.sum(grad_u, axis=0, keepdims=True), jnp.sum(grad_v, axis=0, keepdims=True)))
        r.grad_query[rows, lanes] = mm(flip_low, (grad_u + grad_v).astype(BF16)).astype(BF16)
    r.small[0:1, lanes] = sum(b[0] for b in bias)
    r.small[1:2, lanes] = sum(b[1] for b in bias)
    for par in range(2):
        feats = pair_lanes(p, par * 64, 64)
        for m, out in enumerate((r.grad_key_t, r.grad_value_t, r.grad_place_t)):
            out[feats, :] = sums[par * 3 + m].astype(BF16)


def pair_weights(p, seg, r, base):
    lanes = pair_lanes(p)
    grad_query_t = r.grad_query[:, lanes].astype(F32).T.astype(BF16)
    r.total[rows_at(base, 128)] = mm(grad_query_t, r.normed[seg : 2 * seg]).astype(BF16)
    r.total[rows_at(base + 128, 128)] = mm(r.grad_key_t[lanes, :], r.normed[...]).astype(BF16)
    r.total[rows_at(base + 256, 128)] = mm(r.grad_value_t[lanes, :], r.normed[...]).astype(BF16)
    r.total[rows_at(base + 384, 128)] = mm(r.grad_place_t[lanes, :], r.table[...]).astype(BF16)


def project_places(r):
    r.place[...] = mm(r.table[...], r.w_rel[...]).astype(BF16)


def project_memory(rows, r):
    unit, unused = normalize(r.memory[rows].astype(F32))
    low = (unit * r.vec("gain_one") + r.vec("shift_one")).astype(BF16)
    r.normed[rows] = low
    r.key[rows] = mm(low, r.w_key[...]).astype(BF16)
    r.value[rows] = mm(low, r.w_value[...]).astype(BF16)


def project_segments(n, seg, r):
    rows, keys, unused = query_block(n, seg)
    places = slice(keys - HALF, keys)
    unit, unused = normalize(r.pooled[rows])
    low = (unit * r.vec("gain_one") + r.vec("shift_one")).astype(BF16)
    r.normed[places] = low
    query = mm(low, r.w_query[...])
    scale = 0.125
    r.query_u[rows] = (query + r.vec("bias_u")).astype(BF16) * jnp.asarray(scale, BF16)
    r.query_v[rows] = (query + r.vec("bias_v")).astype(BF16) * jnp.asarray(scale, BF16)
    r.key[places] = mm(low, r.w_key[...]).astype(BF16)
    r.value[places] = mm(low, r.w_value[...]).astype(BF16)


def feed_forward_in(n, r):
    rows = slice(n * HALF, (n + 1) * HALF)
    residual = r.pooled[rows] + mm(r.mixed[rows], r.w_out[...])
    r.residual[rows] = residual
    unit, unused = normalize(residual)
    r.normed_two[rows] = (unit * r.vec("gain_two") + r.vec("shift_two")).astype(BF16)

    for m in range(r.w_up.shape[1] // 512):
        cols = slice(m * 512, (m + 1) * 512)
        inner = mm(r.normed_two[rows], r.w_up[:, cols]) + r.bias_up[0:1, cols]
        gate, slope = gelu_parts(inner)
        r.hidden[rows, cols] = (inner * gate).astype(BF16)
        r.slope[rows, cols] = slope.astype(BF16)


def feed_forward_back(n, r):
    cols = slice(n * 512, (n + 1) * 512)
    r.total[rows_at(BASES[n], 512)] = mm(r.grad_down_t[...], r.hidden[:, cols]).astype(BF16)
    grad_hidden = mm_nt(r.grad_down[...], r.w_down[cols, :])
    low = (grad_hidden * r.slope[:, cols].astype(F32)).astype(BF16)
    r.grad_inner[:, cols] = low
    r.small[7 + n : 8 + n, :] = jnp.sum(low.astype(F32), axis=0, keepdims=True)
    r.total[rows_at(BASES[n] + 512, 512)] = mm(r.normed_two_t[...], low).astype(BF16)


def middle_back(r, base):
    grad_normed = mm_nt(r.grad_inner[...], r.w_up[...])
    unit, inv = normalize(r.residual[...])
    r.small[4:5, :] = jnp.sum(grad_normed * unit, axis=0, keepdims=True)
    r.small[5:6, :] = jnp.sum(grad_normed, axis=0, keepdims=True)
    grad = r.grad_output[...] + norm_back(grad_normed, unit, inv, r.vec("gain_two"))
    r.grad_residual[...] = grad
    low = grad.astype(BF16)
    mixed = r.mixed[...]
    r.total[rows_at(base, 512)] = mm(mixed.astype(F32).T.astype(BF16), low).astype(BF16)
    grad_mixed = (mm_nt(low, r.w_out[...]) * r.scale[...]).astype(BF16)
    r.grad_mixed_t[...] = grad_mixed.astype(F32).T.astype(BF16)
    flip_low = flip_matrix()
    r.grad_mixed[...] = flip(flip_low, grad_mixed)
    r.mixed_flip[...] = flip(flip_low, mixed)
    r.query_u_t[...] = flip(flip_low, r.query_u[...]).astype(F32).T.astype(BF16)
    r.query_v_t[...] = flip(flip_low, r.query_v[...]).astype(F32).T.astype(BF16)


def first_back(seg, r):
    grad_key = r.grad_key_t[...].astype(F32).T.astype(BF16)
    grad_value = r.grad_value_t[...].astype(F32).T.astype(BF16)
    grad_normed = mm_nt(r.grad_query[...], r.w_query[...])
    grad_normed += mm_nt(grad_key[seg:], r.w_key[...])
    grad_normed += mm_nt(grad_value[seg:], r.w_value[...])
    grad_mem = mm_nt(grad_key[:seg], r.w_key[...]) + mm_nt(grad_value[:seg], r.w_value[...])
    unit, inv = normalize(r.pooled[...])
    unit_mem, unused = normalize(r.memory[...].astype(F32))
    r.small[2:3, :] = jnp.sum(grad_normed * unit + grad_mem * unit_mem, axis=0, keepdims=True)
    r.small[3:4, :] = jnp.sum(grad_normed + grad_mem, axis=0, keepdims=True)
    return r.grad_residual[...] + norm_back(grad_normed, unit, inv, r.vec("gain_one"))


QUIET = 384
BACK_PARTS = 8
KEPT_DURING = (18, 9, 14)


def sine_table(count, width):
    freqs = np.exp(np.arange(width // 2) * (-2.0 * math.log(10000.0) / width))
    angles = np.arange(count)[::-1, None] * freqs[None, :]
    return np.concatenate([np.sin(angles), np.cos(angles)], axis=1).astype(jnp.bfloat16)


def span_columns(lengths, low):
    seg = lengths.shape[1]
    lens = lengths.astype(F32).astype(BF16)
    row, col = ramp((seg - low, seg), 0) + low, ramp((seg - low, seg), 1)
    upto = jnp.where(col <= row, 1.0, 0.0).astype(BF16)
    same = jnp.where(col == row, 1.0, 0.0).astype(BF16)
    return mm_nt(upto, lens), mm_nt(same, lens)


def column(value, n):
    return jnp.sum(jnp.where(ramp(value.shape, 1) == n, value, 0.0), axis=1, keepdims=True)


WEIGHTS = ("w_query", "w_key", "w_value", "w_rel", "w_out", "w_up", "w_down")


def layer_scratch(seg, width, hidden):
    def low(*shape):
        return pltpu.VMEM(shape, BF16)

    def full(*shape):
        return pltpu.VMEM(shape, F32)

    return dict(
        table=low(2 * seg, width),
        w_query=low(width, width),
        w_key=low(width, width),
        w_value=low(width, width),
        w_rel=low(width, width),
        w_out=low(width, width),
        w_up=low(width, hidden),
        w_down=low(hidden, width),
        memory=low(seg, width),
        pooled=full(seg, width),
        normed=low(2 * seg, width),
        key=low(2 * seg, width),
        value=low(2 * seg, width),
        place=low(2 * seg, width),
        query_u=low(seg, width),
        query_v=low(seg, width),
        mixed=low(seg, width),
        probs=low(8, seg, 2 * seg),
        scale=full(seg, width),
        residual=full(seg, width),
        normed_two=low(seg, width),
        normed_two_t=low(width, seg),
        hidden=low(seg, hidden),
        slope=low(seg, hidden),
        grad_inner=low(seg, hidden),
        grad_output=full(seg, width),
        grad_down=low(seg, width),
        grad_down_t=low(width, seg),
        low_rows=low(seg, width),
        out_rows=low(seg, width),
        chars_quiet=low(QUIET, width),
        chars_parts=low(7, seg - QUIET, width),
        grads_quiet=low(QUIET, width),
        grads_parts=low(7, seg - QUIET, width),
        total=low(BASES[-1], width),
        land_0=low(BASES[-1] >> 1, width),
        land_1=low(BASES[-1] >> 2, width),
        land_2=low(BASES[-1] >> 3, width),
        land_3=low(BASES[-1] >> 4, width),
        land_4=low(BASES[-1] >> 5, width),
        bias_up=full(1, hidden),
        vectors=full(16, width),
        small=full(16, width),
        small_sum=full(5, 16, width),
        small_land=full(5, 16, width),
        load_sem=pltpu.SemaphoreType.DMA((len(WEIGHTS) + 1,)),
        stage_sem=pltpu.SemaphoreType.DMA((2, 4)),
        memory_send=pltpu.SemaphoreType.DMA((4,)),
        memory_recv=pltpu.SemaphoreType.DMA((4,)),
        quiet_send=pltpu.SemaphoreType.DMA((2, 4, 2)),
        quiet_recv=pltpu.SemaphoreType.DMA((2, 2)),
        parts_send=pltpu.SemaphoreType.DMA((2, 3)),
        parts_recv=pltpu.SemaphoreType.DMA((2, 3)),
        kept_send=pltpu.SemaphoreType.DMA((6,)),
        kept_recv=pltpu.SemaphoreType.DMA((4,)),
        back_send=pltpu.SemaphoreType.DMA((2, 5)),
        back_recv=pltpu.SemaphoreType.DMA((2, 2, 4)),
        sum_send=pltpu.SemaphoreType.DMA((len(PIECES),)),
        sum_recv=pltpu.SemaphoreType.DMA((len(PIECES), STEPS - 1)),
        small_send=pltpu.SemaphoreType.DMA((5,)),
        small_recv=pltpu.SemaphoreType.DMA((5,)),
        small_sem=pltpu.SemaphoreType.DMA,
        store_sem=pltpu.SemaphoreType.DMA((len(PIECES),)),
    )


class Rows:
    def __init__(self, r, place, way, source, stage, quiet, parts):
        self.r, self.p, self.way = r, place, way
        self.source, self.stage, self.quiet, self.parts = source, stage, quiet, parts

    def load(self, n):
        cols = pl.ds(pl.multiple_of(n * 512, 512), 512)
        return pltpu.make_async_copy(self.source.at[n], self.stage.at[:, cols], self.r.stage_sem.at[self.way, n])

    def quiet_copy(self, to, part):
        r = self.r
        span = pl.ds(0, HALF) if part == 0 else pl.ds(HALF, QUIET - HALF)
        src, dst = self.source.at[to, span], self.quiet.at[span]
        if to == 0:
            return pltpu.make_async_copy(src, dst, r.quiet_send.at[self.way, 0, part])
        return remote(src, dst, r.quiet_send.at[self.way, to, part], r.quiet_recv.at[self.way, part], (self.p.s, to))

    def start_quiet(self):
        @pl.when(self.p.b == 0)
        def _():
            for part in range(2):
                for to in (2, 3, 1, 0):
                    self.quiet_copy(to, part).start()

    def wait_quiet(self, part):
        @pl.when(self.p.b == 0)
        def _():
            self.quiet_copy(0, part).wait()

        @pl.when(self.p.b != 0)
        def _():
            self.quiet_copy(1, part).wait_recv()

    def parts_copy(self, n):
        src, dst, to = ((3, 1, self.p.core()), (4, 5, self.p.core()), (6, 2, self.p.across()))[n]
        return remote(
            self.parts.at[src],
            self.parts.at[dst],
            self.r.parts_send.at[self.way, n],
            self.r.parts_recv.at[self.way, n],
            to,
        )

    def part(self, to, ends, lens):
        self.load(to).wait()
        cols = pl.ds(pl.multiple_of(to * 512, 512), 512)
        chosen = pool_matrix(column(ends, to), column(lens, to), self.p.b * 512, 512)
        return mm(chosen, self.stage[:, cols])

    def start_parts(self, ends, lens):
        b, sibling, away = self.p.b, self.p.core()[1], self.p.across()[1]
        self.parts[4] = self.part(away + sibling - b, ends, lens).astype(BF16)
        self.parts_copy(1).start()
        self.parts[3] = self.part(sibling, ends, lens).astype(BF16)
        self.parts_copy(0).start()
        self.parts[6] = self.part(away, ends, lens).astype(BF16)
        self.parts[0] = self.part(b, ends, lens).astype(BF16)

    def join_parts(self):
        self.parts_copy(1).wait_recv()
        self.parts[6] = (self.parts[6].astype(F32) + self.parts[5].astype(F32)).astype(BF16)
        self.parts_copy(2).start()

    def wait_parts(self):
        self.parts_copy(0).wait_recv()
        self.parts_copy(2).wait_recv()
        return sum(self.parts[n].astype(F32) for n in range(3))

    def wait_sent(self):
        for n in range(3):
            self.parts_copy(n).wait_send()

        @pl.when(self.p.b == 0)
        def _():
            for part in range(2):
                for to in (1, 2, 3):
                    self.quiet_copy(to, part).wait_send()

    def back(self, rows, quiet_out, loud_out):
        self.rows, self.quiet_out, self.loud_out = rows, quiet_out, loud_out
        return self

    def loud_rows(self):
        return self.rows.at[pl.ds(QUIET, self.rows.shape[0] - QUIET)]

    def quiet_rows(self):
        return self.rows.at[pl.ds(0, QUIET)]

    def loud_copy(self, n, slot):
        r, p, way = self.r, self.p, self.way
        src = self.loud_out.at[slot] if n == 2 else self.loud_rows()
        to = p.across() if n == 1 else p.core()
        return remote(src, self.loud_out.at[slot], r.back_send.at[way, n], r.back_recv.at[way, 0, slot], to)

    def quiet_back(self, slot, start=0, size=QUIET):
        r, way = self.r, self.way
        span = pl.ds(start, size)
        return remote(
            self.rows.at[span],
            self.quiet_out.at[slot, span],
            r.back_send.at[way, 3],
            r.back_recv.at[way, 1, slot],
            (self.p.s, 0),
        )

    def own_copies(self):
        r, p, way = self.r, self.p, self.way
        loud = pltpu.make_async_copy(self.loud_rows(), self.loud_out.at[p.b], r.back_send.at[way, 4])
        quiet = pltpu.make_async_copy(self.quiet_rows(), self.quiet_out.at[0], r.back_send.at[way, 3])
        return loud, quiet

    def start_back(self):
        p = self.p
        loud, quiet = self.own_copies()
        self.loud_copy(1, p.b).start()
        self.loud_copy(0, p.b).start()
        pl.when(p.b == 0)(quiet.start)
        loud.start()

    def start_quiet_back(self, n):
        size = QUIET // BACK_PARTS
        pl.when(self.p.b != 0)(self.quiet_back(self.p.b, n * size, size).start)

    def pass_on(self):
        away = self.p.across()[1]
        self.loud_copy(1, away).wait_recv()
        self.loud_copy(2, away).start()

    def wait_back(self):
        p = self.p
        sibling, away = p.core()[1], p.across()[1]
        loud, quiet = self.own_copies()
        for n in (0, 1):
            self.loud_copy(n, p.b).wait_send()
        self.loud_copy(2, away).wait_send()
        loud.wait()
        pl.when(p.b != 0)(self.quiet_back(p.b).wait_send)
        pl.when(p.b == 0)(quiet.wait)
        self.loud_copy(0, sibling).wait_recv()
        self.loud_copy(2, away + sibling - p.b).wait_recv()

        @pl.when(p.b == 0)
        def _():
            for n in (1, 2, 3):
                self.quiet_back(n).wait_recv()


class Kept:
    def __init__(self, r, place, chars, kept):
        self.r, self.p, self.chars, self.kept = r, place, chars, kept
        self.count = kept.shape[1]

    def rows(self, to):
        return self.r.low_rows.at[pl.ds(to * self.count, self.count)]

    def late(self, to, slot):
        r = self.r
        return remote(self.rows(to), self.kept.at[slot], r.kept_send.at[4 + to - 2], r.kept_recv.at[slot], (self.p.s, to))

    def late_own(self, to):
        return pltpu.make_async_copy(self.rows(to), self.kept.at[to], self.r.kept_send.at[4 + to - 2])

    def early(self, slot):
        r = self.r
        src = self.chars.at[slot, pl.ds(self.count, self.count)]
        return remote(src, self.kept.at[slot], r.kept_send.at[slot], r.kept_recv.at[slot], (self.p.s, 1))

    def early_own(self, slot):
        src = self.chars.at[slot, pl.ds(0, self.count)]
        return pltpu.make_async_copy(src, self.kept.at[slot], self.r.kept_recv.at[slot])

    def start_late(self, to):
        pl.when(self.p.b != to)(self.late(to, self.p.b).start)
        pl.when(self.p.b == to)(self.late_own(to).start)

    def start_early(self):
        @pl.when(self.p.b == 0)
        def _():
            for slot in range(4):
                self.early_own(slot).start()
                self.early(slot).start()

    def wait(self):
        b = self.p.b

        @pl.when(b == 0)
        def _():
            for slot in range(4):
                self.early_own(slot).wait()
                self.early(slot).wait_send()

        @pl.when(b == 1)
        def _():
            for slot in range(4):
                self.early(slot).wait_recv()

        for to in (2, 3):
            pl.when(b != to)(self.late(to, b).wait_send)

            @pl.when(b == to)
            def _():
                self.late_own(to).wait()
                for slot in range(4):
                    if slot != to:
                        self.late(to, slot).wait_recv()


class Small:
    def __init__(self, r, place):
        self.r, self.p = r, place

    def source(self, step):
        return self.r.small if step == 0 else self.r.small_sum.at[step - 1]

    def copy(self, step):
        r, p = self.r, self.p
        to = p.core() if step == 0 else p.pair(AXES[step - 1])
        return remote(self.source(step), r.small_land.at[step], r.small_send.at[step], r.small_recv.at[step], to)

    def start(self, step):
        self.copy(step).start()

    def finish(self, step):
        self.copy(step).wait()
        self.r.small_sum[step] = self.source(step)[...] + self.r.small_land[step]


def layer_kernel(names, chars, lengths, memory, grad_out, *rest):
    count = len(VECTORS) + 1 + len(WEIGHTS)
    vectors, table, weights = rest[: len(VECTORS)], rest[len(VECTORS)], rest[len(VECTORS) + 1 : count]
    kept, out_quiet, out_loud, grad_quiet, grad_loud, total_out, small_out = rest[count : count + 7]
    r = types.SimpleNamespace(**dict(zip(names, rest[count + 7 :])))
    p = Place()
    seg, width = r.pooled.shape
    r.grad_residual, r.grad_mixed, r.grad_rows = r.grad_output, r.grad_down, r.normed_two
    for n, name in enumerate(("mixed_flip", "query_u_t", "query_v_t", "grad_mixed_t")):
        setattr(r, name, r.slope.at[:, n * width : (n + 1) * width])
    r.grad_key_t, r.grad_value_t = r.hidden.at[:, : 2 * seg], r.hidden.at[:, 2 * seg :]
    r.grad_place_t, r.grad_query = r.grad_inner.at[:, : 2 * seg], r.grad_inner.at[:, 2 * seg : 3 * seg]
    loads = [
        pltpu.make_async_copy(src, dst, r.load_sem.at[n])
        for n, (src, dst) in enumerate(
            zip((*weights, table), [getattr(r, name) for name in WEIGHTS] + [r.table])
        )
    ]
    chars_rows = Rows(r, p, 0, chars, r.hidden, r.chars_quiet, r.chars_parts).back(r.out_rows, out_quiet, out_loud)
    grads_rows = Rows(r, p, 1, grad_out, r.grad_inner, r.grads_quiet, r.grads_parts).back(
        r.grad_rows, grad_quiet, grad_loud
    )
    for n in range(4):
        chars_rows.load(n).start()
    for n in range(4):
        grads_rows.load(n).start()
    for copy in loads:
        copy.start()
    for n, name in enumerate(VECTORS):
        value = vectors[n][...].astype(F32)
        if name == "bias_up":
            r.bias_up[...] = value.reshape(1, -1)
        elif value.ndim == 2:
            r.vectors[n : n + 1, :] = jnp.concatenate([value[h : h + 1, :] for h in range(value.shape[0])], axis=1)
        else:
            r.vectors[n : n + 1, :] = value.reshape(1, -1)
    r.vec = lambda name: r.vectors[VECTORS.index(name) : VECTORS.index(name) + 1, :]

    barrier = pltpu.get_barrier_semaphore()
    others = [p.group(1), p.group(2), p.group(3), p.pair("y"), p.pair("near"), p.pair("far")]
    for other in others:
        pl.semaphore_signal(barrier, inc=1, device_id=other, device_id_type=MESH)
    pl.semaphore_wait(barrier, len(others))

    rows = memory.shape[1]

    def memory_copy(k, slot):
        to = (p.b + k) % 4
        return remote(
            memory.at[to], r.memory.at[rows_at(slot * rows, rows)], r.memory_send.at[k], r.memory_recv.at[slot], p.group(k)
        )

    own_memory = pltpu.make_async_copy(memory.at[p.b], r.memory.at[rows_at(p.b * rows, rows)], r.memory_send.at[0])
    for k in (2, 3, 1):
        memory_copy(k, p.b).start()
    own_memory.start()
    chars_rows.start_quiet()
    ends, lens = span_columns(lengths[...], QUIET)
    chars_rows.start_parts(ends, lens)
    for copy in loads:
        copy.wait()
    project_places(r)
    chars_rows.join_parts()
    grads_rows.start_quiet()
    grads_rows.start_parts(ends, lens)
    own_memory.wait()
    memory_copy(1, p.core()[1]).wait_recv()
    project_memory(rows_at(p.x * 2 * rows, 2 * rows), r)
    for slot in (2 * (1 - p.x), 2 * (1 - p.x) + 1):
        memory_copy(1, slot).wait_recv()
    project_memory(rows_at((1 - p.x) * 2 * rows, 2 * rows), r)
    own_lens = column(lens, p.b)

    def forward(block):
        project_segments(block, seg, r)
        attend(block, seg, r)
        feed_forward_in(block, r)

    chars_rows.wait_quiet(0)
    r.pooled[0:HALF] = chars_rows.quiet[0:HALF].astype(F32)
    forward(0)
    grads_rows.join_parts()
    chars_rows.wait_quiet(1)
    r.pooled[HALF:QUIET] = chars_rows.quiet[HALF:QUIET].astype(F32)
    r.pooled[QUIET:seg] = chars_rows.wait_parts() / own_lens
    r.low_rows[...] = r.pooled[...].astype(BF16)

    forward(1)
    grads_rows.wait_quiet(0)
    grads_rows.wait_quiet(1)
    r.grad_output[0:QUIET] = grads_rows.quiet[...].astype(F32)
    r.grad_output[QUIET:seg] = grads_rows.wait_parts()
    low = r.grad_output[...].astype(BF16)
    r.grad_down[...] = low
    r.grad_down_t[...] = low.astype(F32).T.astype(BF16)
    r.normed_two_t[...] = r.normed_two[...].astype(F32).T.astype(BF16)
    r.small[...] = jnp.zeros(r.small.shape, F32)
    r.small[6:7, :] = jnp.sum(low.astype(F32), axis=0, keepdims=True)

    land = [getattr(r, f"land_{n}") for n in range(5)]
    sums = Sum(p, r.total, land, total_out, r.sum_send, r.sum_recv, r.store_sem)

    rows_kept = Kept(r, p, chars, kept)

    def take(n):
        if n == KEPT_DURING[0]:
            rows_kept.start_early()
        for to in (2, 3):
            if n == KEPT_DURING[to - 1]:
                rows_kept.start_late(to)
        for part, at in enumerate(BACK_DURING):
            if at == n:
                chars_rows.start_quiet_back(part)
        for k, step in DURING[n]:
            sums.step(k, step)

    def between(pair, unit):
        for n in range(4):
            at = n * 5 + 6 + unit
            if DURING[at] or at in BACK_DURING or at in KEPT_DURING:
                pl.when(pair == n)(functools.partial(take, at))

    for n in range(4):
        feed_forward_back(n, r)
        take(n)
    r.out_rows[...] = (r.residual[...] + (mm(r.hidden[...], r.w_down[...]) + r.vec("bias_down"))).astype(BF16)
    chars_rows.start_back()
    take(4)
    middle_back(r, BASES[4])
    take(5)

    def back(n, carry):
        attend_back_pair(n, seg, r, functools.partial(between, n))
        pair_weights(n, seg, r, BASES[5] + n * PIECES[5][0])
        between(n, 4)
        return carry

    lax.fori_loop(0, 4, back, 0)
    grad_pooled = first_back(seg, r)
    r.grad_rows[0:QUIET] = grad_pooled[:QUIET].astype(BF16)
    r.grad_rows[QUIET:seg] = (grad_pooled[QUIET:] / own_lens).astype(BF16)
    grads_rows.start_back()
    small = Small(r, p)
    small_store = pltpu.make_async_copy(r.small_sum.at[4], small_out, r.small_sem)
    small.start(0)
    take(26)
    every = len(AFTER) // 12
    for n, (k, step) in enumerate(AFTER):
        for part, at in enumerate(BACK_AFTER):
            if at == n:
                grads_rows.start_quiet_back(part)
        if n % every == every - 1 and n // every < 10:
            at = n // every
            if at % 2 == 1:
                small.finish(at // 2)
                if at // 2 < 4:
                    small.start(at // 2 + 1)
                else:
                    small_store.start()
            if at == 4:
                chars_rows.pass_on()
            if at == 8:
                grads_rows.pass_on()
        sums.step(k, step)
    for k in (1, 2, 3):
        memory_copy(k, p.b).wait_send()
    rows_kept.wait()
    chars_rows.wait_sent()
    grads_rows.wait_sent()
    chars_rows.wait_back()
    grads_rows.wait_back()
    small_store.wait()


def spread_kernel(
    lengths, chars, grad_out, rows, out_quiet, out_loud, grad_quiet, grad_loud, wide, flat, pairs, small,
    out_chars, grad_chars, kept, w_query, w_key, w_value, w_rel, w_out, w_up, w_down, bias_u, bias_v, *vectors,
):
    n = pl.program_id(0)
    b = lax.axis_index("blk")
    places = chars.shape[1]
    seg = lengths.shape[1]
    lens = lengths[...].astype(F32).astype(BF16)
    row, col = ramp((seg - QUIET, seg), 0) + QUIET, ramp((seg - QUIET, seg), 1)
    upto = jnp.where(col <= row, 1.0, 0.0).astype(BF16)
    same = jnp.where(col == row, 1.0, 0.0).astype(BF16)
    pick = ramp((lengths.shape[0], seg - QUIET), 0) == n
    end = jnp.sum(jnp.where(pick, mm_nt(lens, upto), 0.0), axis=0, keepdims=True)
    length = jnp.sum(jnp.where(pick, mm_nt(lens, same), 0.0), axis=0, keepdims=True)
    place = (ramp((places, seg - QUIET), 0) + b * places).astype(F32)
    chosen = jnp.where((place < end) & (place >= end - length), 1.0, 0.0).astype(BF16)
    first = b == 0
    kept[...] = rows[...]
    for source, quiet, loud, out in (
        (chars, out_quiet, out_loud, out_chars),
        (grad_out, grad_quiet, grad_loud, grad_chars),
    ):
        spread = mm(chosen, loud[0])
        whole = source[0].astype(F32) + spread
        out[0, QUIET:places] = whole[QUIET:].astype(out.dtype)
        out[0, 0:QUIET] = (whole[:QUIET] + jnp.where(first, quiet[0].astype(F32), 0.0)).astype(out.dtype)
    w_down[...] = wide[0:512].astype(F32).T
    w_up[...] = wide[512:1024].astype(F32)
    w_out[...] = flat[...].astype(F32)
    for m, out in enumerate((w_query, w_key, w_value, w_rel)):
        out[...] = pairs[m * 128 : (m + 1) * 128].astype(F32).T
    for m, out in enumerate((bias_u, bias_v)):
        out[...] = jnp.concatenate([small[m : m + 1, h * 64 : (h + 1) * 64] for h in range(8)], axis=0)
    for m, out in enumerate(vectors[:4]):
        out[...] = small[2 + m : 3 + m, :]
    vectors[4][...] = jnp.concatenate([small[m : m + 1, :] for m in range(7, 11)], axis=1)
    vectors[5][...] = small[6:7, :]


def shards_whole(
    chars, seg_lengths, memory, grad_out, w_query, w_key, w_value, w_rel, w_out, w_up, w_down,
    bias_u, bias_v, gain_one, shift_one, gain_two, shift_two, bias_up, bias_down,
):
    count, places, width = chars.shape
    seg, hidden = seg_lengths.shape[1], w_up.shape[1]
    rows = memory.shape[1]
    table = jnp.asarray(sine_table(2 * seg, width))
    scratch = layer_scratch(seg, width, hidden)
    anywhere, near = pl.BlockSpec(memory_space=pl.ANY), pl.BlockSpec(memory_space=pltpu.VMEM)
    loud = seg - QUIET
    kept, out_quiet, out_loud, grad_quiet, grad_loud, total, small = pl.pallas_call(
        functools.partial(layer_kernel, tuple(scratch)),
        out_shape=[
            jax.ShapeDtypeStruct((count, rows, width), BF16),
            jax.ShapeDtypeStruct((count, QUIET, width), BF16),
            jax.ShapeDtypeStruct((count, loud, width), BF16),
            jax.ShapeDtypeStruct((count, QUIET, width), BF16),
            jax.ShapeDtypeStruct((count, loud, width), BF16),
            jax.ShapeDtypeStruct((BASES[-1], width), BF16),
            jax.ShapeDtypeStruct((16, width), F32),
        ],
        in_specs=[anywhere, near, anywhere, anywhere] + [near] * len(VECTORS) + [anywhere] * 8,
        out_specs=[anywhere] * 7,
        scratch_shapes=list(scratch.values()),
        compiler_params=pltpu.CompilerParams(
            collective_id=0, has_side_effects=True, vmem_limit_bytes=VMEM_BYTES
        ),
        name="layer",
    )(
        chars, seg_lengths, memory, grad_out,
        bias_u, bias_v, gain_one, shift_one, gain_two, shift_two, bias_up, bias_down, table,
        w_query, w_key, w_value, w_rel, w_out, w_up, w_down,
    )

    def block(shape, index):
        return pl.BlockSpec(shape, index)

    def each(*shape):
        return block((1, *shape), lambda n: (n, 0, 0))

    def whole(*shape):
        return block(shape, lambda n: (0, 0))

    vector = [(1, width)] * 4 + [(1, hidden), (1, width)]
    outs = pl.pallas_call(
        spread_kernel,
        grid=(count,),
        out_shape=[
            jax.ShapeDtypeStruct(chars.shape, BF16),
            jax.ShapeDtypeStruct(chars.shape, F32),
            jax.ShapeDtypeStruct(memory.shape, BF16),
            *[jax.ShapeDtypeStruct((width, width), F32)] * 5,
            jax.ShapeDtypeStruct((width, hidden), F32),
            jax.ShapeDtypeStruct((hidden, width), F32),
            *[jax.ShapeDtypeStruct(bias_u.shape, F32)] * 2,
            *[jax.ShapeDtypeStruct(shape, F32) for shape in vector],
        ],
        in_specs=[
            whole(*seg_lengths.shape),
            each(places, width),
            each(places, width),
            each(rows, width),
            each(QUIET, width),
            each(loud, width),
            each(QUIET, width),
            each(loud, width),
            block((1024, width), lambda n: (n, 0)),
            block((128, width), lambda n: (BASES[4] // 128 + n, 0)),
            block((512, width), lambda n: (BASES[5] // 512 + n, 0)),
            whole(16, width),
        ],
        out_specs=[
            each(places, width),
            each(places, width),
            each(rows, width),
            *[block((width, 128), lambda n: (0, n))] * 4,
            block((128, width), lambda n: (n, 0)),
            block((width, 512), lambda n: (0, n)),
            block((512, width), lambda n: (n, 0)),
            *[whole(*bias_u.shape)] * 2,
            *[whole(*shape) for shape in vector],
        ],
        compiler_params=pltpu.CompilerParams(vmem_limit_bytes=VMEM_BYTES),
        name="spread",
    )(seg_lengths, chars, grad_out, kept, out_quiet, out_loud, grad_quiet, grad_loud, total, total, total, small)
    return (*outs[:12], *[v.reshape(-1) for v in outs[12:]])


VMEM_BYTES = 64 * 2**20 - 2**16


def fits_whole(mesh):
    return dict(mesh.shape) == {"seq": 8, "blk": 4}


def layer_norm(value, gain, shift):
    center = value - jnp.mean(value, axis=-1, keepdims=True)
    spread = jnp.mean(center * center, axis=-1, keepdims=True)
    return center * lax.rsqrt(spread + 1e-05) * gain + shift


def angle_tables(places, feature_width):
    freqs = jnp.exp(
        jnp.arange(feature_width // 2, dtype=jnp.float32)
        * (-2.0 * math.log(10000.0) / feature_width)
    )
    angles = places[:, None] * freqs[None, :]
    return (jnp.sin(angles), jnp.cos(angles))


def smooth_gate(value):
    return jax.nn.gelu(value, approximate=False)


def segment_ids(seg_end, char_places):
    return jnp.sum((seg_end[:, None, :] <= char_places[None, :, None]).astype(jnp.int32), axis=2)


def shards(
    chars,
    seg_lengths,
    memory,
    grad_out,
    w_query,
    w_key,
    w_value,
    w_rel,
    w_out,
    w_up,
    w_down,
    bias_u,
    bias_v,
    gain_one,
    shift_one,
    gain_two,
    shift_two,
    bias_up,
    bias_down,
):
    blk_index = lax.axis_index("blk")
    seq_local, char_rows, feature_width = chars.shape
    seg_rows = memory.shape[1]
    seg_count = seg_lengths.shape[1]
    head_count, head_dim = bias_u.shape
    half_width = feature_width // 2
    score_scale = head_dim ** (-0.5)
    seg_start = blk_index * seg_rows
    gain_one_f = gain_one.astype(jnp.float32)
    shift_one_f = shift_one.astype(jnp.float32)
    gain_two_f = gain_two.astype(jnp.float32)
    shift_two_f = shift_two.astype(jnp.float32)
    seg_end = jnp.cumsum(seg_lengths, axis=1)
    char_places = blk_index * char_rows + jnp.arange(char_rows, dtype=jnp.int32)
    segment = segment_ids(seg_end, char_places)
    own_lengths = lax.dynamic_slice_in_dim(seg_lengths, seg_start, seg_rows, 1).astype(jnp.float32)
    chars_f = chars.astype(jnp.float32)
    grad_f = grad_out.astype(jnp.float32)

    def full_table(values, ids):
        return jax.ops.segment_sum(values, ids, num_segments=seg_count)

    part_sums = jax.vmap(full_table)(chars_f, segment)
    pooled_sum = lax.psum_scatter(part_sums, "blk", scatter_dimension=1, tiled=True)
    pooled = pooled_sum / own_lengths[:, :, None]
    normed = layer_norm(pooled, gain_one_f, shift_one_f)
    normed_low = normed.astype(jnp.bfloat16)
    memory_f = memory.astype(jnp.float32)
    mem_low = layer_norm(memory_f, gain_one_f, shift_one_f).astype(jnp.bfloat16)
    query_rows = jnp.einsum("sid,de->sie", normed_low, w_query, preferred_element_type=jnp.float32)
    key_local = jnp.stack(
        [
            jnp.einsum("sid,de->sie", mem_low, w_key, preferred_element_type=jnp.float32),
            jnp.einsum("sid,de->sie", normed_low, w_key, preferred_element_type=jnp.float32),
        ],
        axis=1,
    ).astype(jnp.bfloat16)
    value_local = jnp.stack(
        [
            jnp.einsum("sid,de->sie", mem_low, w_value, preferred_element_type=jnp.float32),
            jnp.einsum("sid,de->sie", normed_low, w_value, preferred_element_type=jnp.float32),
        ],
        axis=1,
    ).astype(jnp.bfloat16)
    key_all, value_all = (
        lax.all_gather(key_local, "blk", axis=2, tiled=True),
        lax.all_gather(value_local, "blk", axis=2, tiled=True),
    )
    key_heads = key_all.reshape(seq_local, 2 * seg_count, head_count, head_dim)
    value_heads = value_all.reshape(seq_local, 2 * seg_count, head_count, head_dim)
    query_u = (
        (query_rows + bias_u.astype(jnp.float32).reshape(-1))
        .astype(jnp.bfloat16)
        .reshape(seq_local, seg_rows, head_count, head_dim)
    )
    query_v = (
        (query_rows + bias_v.astype(jnp.float32).reshape(-1))
        .astype(jnp.bfloat16)
        .reshape(seq_local, seg_rows, head_count, head_dim)
    )
    w_rel_heads = w_rel.reshape(feature_width, head_count, head_dim)
    rel_coeff = jnp.einsum(
        "sihe,fhe->sihf", query_v, w_rel_heads, preferred_element_type=jnp.float32
    )
    sin_all, cos_all = angle_tables(jnp.arange(2 * seg_count).astype(jnp.float32), feature_width)
    key_pos = jnp.concatenate([cos_all, sin_all], axis=-1).astype(jnp.bfloat16)
    query_index = seg_count + seg_start + jnp.arange(seg_rows, dtype=jnp.int32)
    sin_q, cos_q = angle_tables(query_index.astype(jnp.float32), feature_width)
    sin_query = sin_q[None, :, None, :]
    cos_query = cos_q[None, :, None, :]
    coeff_sin = rel_coeff[..., :half_width]
    coeff_cos = rel_coeff[..., half_width:]
    query_pos = jnp.concatenate(
        [
            coeff_sin * sin_query + coeff_cos * cos_query,
            coeff_cos * sin_query - coeff_sin * cos_query,
        ],
        axis=-1,
    ).astype(jnp.bfloat16)
    allowed = jnp.arange(2 * seg_count, dtype=jnp.int32)[None, :] <= query_index[:, None]

    def score_block():
        raw_scores = (
            jnp.einsum("sihe,sjhe->shij", query_u, key_heads, preferred_element_type=jnp.float32)
            + jnp.einsum("sihf,jf->shij", query_pos, key_pos, preferred_element_type=jnp.float32)
        ) * score_scale
        return jnp.where(allowed[None, None], raw_scores, -1e30)

    scores = score_block()
    row_top = jnp.max(scores, axis=-1, keepdims=True)
    expo = jnp.exp(scores - row_top)
    row_total = jnp.sum(expo, axis=-1, keepdims=True)
    log_total = row_top + jnp.log(row_total)
    att_probs = (expo / row_total).astype(jnp.bfloat16)
    att_mixed = jnp.einsum(
        "shij,sjhe->sihe", att_probs, value_heads, preferred_element_type=jnp.float32
    )
    mixed_low = att_mixed.reshape(seq_local, seg_rows, feature_width).astype(jnp.bfloat16)
    residual = pooled + jnp.einsum(
        "sid,de->sie", mixed_low, w_out, preferred_element_type=jnp.float32
    )
    normed_two = layer_norm(residual, gain_two_f, shift_two_f)
    two_low = normed_two.astype(jnp.bfloat16)
    ffn_inner = jnp.einsum(
        "sid,df->sif", two_low, w_up, preferred_element_type=jnp.float32
    ) + bias_up.astype(jnp.float32)
    hidden_low = smooth_gate(ffn_inner).astype(jnp.bfloat16)
    branch_out = jnp.einsum(
        "sif,fd->sid", hidden_low, w_down, preferred_element_type=jnp.float32
    ) + bias_down.astype(jnp.float32)
    out_low = (residual + branch_out).astype(jnp.bfloat16)
    rows_all = lax.all_gather(out_low, "blk", axis=1, tiled=True)
    picked = jnp.take_along_axis(rows_all, segment[:, :, None], axis=1)
    out_chars = (chars_f + picked.astype(jnp.float32)).astype(jnp.bfloat16)
    new_memory = pooled.astype(jnp.bfloat16)
    grad_table = jax.vmap(full_table)(grad_f, segment)
    grad_output = lax.psum_scatter(grad_table, "blk", scatter_dimension=1, tiled=True)
    grad_down_low = grad_output.astype(jnp.bfloat16)
    grad_bias_down = jnp.sum(grad_down_low.astype(jnp.float32), axis=(0, 1))
    grad_w_down = jnp.einsum(
        "sif,sid->fd", hidden_low, grad_down_low, preferred_element_type=jnp.float32
    )
    grad_hidden = jnp.einsum(
        "sid,fd->sif", grad_down_low, w_down, preferred_element_type=jnp.float32
    )
    unused_value, gate_back = jax.vjp(smooth_gate, ffn_inner)
    grad_inner = gate_back(grad_hidden)[0].astype(jnp.bfloat16)
    grad_bias_up = jnp.sum(grad_inner.astype(jnp.float32), axis=(0, 1))
    grad_w_up = jnp.einsum("sid,sif->df", two_low, grad_inner, preferred_element_type=jnp.float32)
    grad_normed_two = jnp.einsum(
        "sif,df->sid", grad_inner, w_up, preferred_element_type=jnp.float32
    )
    unused_norm, norm_two_back = jax.vjp(layer_norm, residual, gain_two_f, shift_two_f)
    grad_resid_norm, grad_gain_two, grad_shift_two = norm_two_back(grad_normed_two)
    grad_residual = grad_output + grad_resid_norm
    grad_att_low = grad_residual.astype(jnp.bfloat16)
    grad_w_out = jnp.einsum(
        "sid,sie->de", mixed_low, grad_att_low, preferred_element_type=jnp.float32
    )
    grad_mixed = jnp.einsum("sie,de->sid", grad_att_low, w_out, preferred_element_type=jnp.float32)
    grad_mixed = grad_mixed.astype(jnp.bfloat16).reshape(seq_local, seg_rows, head_count, head_dim)
    scores_again = score_block()
    probs_full = jnp.exp(scores_again - log_total)
    probs_low = probs_full.astype(jnp.bfloat16)
    grad_probs = jnp.einsum(
        "sihe,sjhe->shij", grad_mixed, value_heads, preferred_element_type=jnp.float32
    )
    grad_values = jnp.einsum(
        "shij,sihe->sjhe", probs_low, grad_mixed, preferred_element_type=jnp.float32
    )
    prob_delta = jnp.sum(probs_full * grad_probs, axis=-1, keepdims=True)
    grad_scores = (probs_full * (grad_probs - prob_delta)).astype(jnp.bfloat16)
    grad_query_u = (
        jnp.einsum("shij,sjhe->sihe", grad_scores, key_heads, preferred_element_type=jnp.float32)
        * score_scale
    )
    grad_keys = (
        jnp.einsum("shij,sihe->sjhe", grad_scores, query_u, preferred_element_type=jnp.float32)
        * score_scale
    )
    grad_query_pos = (
        jnp.einsum("shij,jf->sihf", grad_scores, key_pos, preferred_element_type=jnp.float32)
        * score_scale
    )
    grad_first = grad_query_pos[..., :half_width]
    grad_second = grad_query_pos[..., half_width:]
    grad_coeff = jnp.concatenate(
        [
            grad_first * sin_query - grad_second * cos_query,
            grad_first * cos_query + grad_second * sin_query,
        ],
        axis=-1,
    ).astype(jnp.bfloat16)
    grad_w_rel = jnp.einsum(
        "sihf,sihe->fhe", grad_coeff, query_v, preferred_element_type=jnp.float32
    ).reshape(feature_width, feature_width)
    grad_query_v = jnp.einsum(
        "sihf,fhe->sihe", grad_coeff, w_rel_heads, preferred_element_type=jnp.float32
    )
    grad_bias_u = jnp.sum(grad_query_u, axis=(0, 1))
    grad_bias_v = jnp.sum(grad_query_v, axis=(0, 1))
    grad_query = (
        (grad_query_u + grad_query_v)
        .reshape(seq_local, seg_rows, feature_width)
        .astype(jnp.bfloat16)
    )
    grad_w_query = jnp.einsum(
        "sid,sie->de", normed_low, grad_query, preferred_element_type=jnp.float32
    )
    grad_normed = jnp.einsum("sie,de->sid", grad_query, w_query, preferred_element_type=jnp.float32)
    key_share, value_share = (
        lax.psum_scatter(
            grad_keys.reshape(seq_local, 2, seg_count, feature_width),
            "blk",
            scatter_dimension=2,
            tiled=True,
        ),
        lax.psum_scatter(
            grad_values.reshape(seq_local, 2, seg_count, feature_width),
            "blk",
            scatter_dimension=2,
            tiled=True,
        ),
    )
    key_low = key_share.astype(jnp.bfloat16)
    value_low = value_share.astype(jnp.bfloat16)
    grad_w_key = jnp.einsum(
        "sid,sie->de", mem_low, key_low[:, 0], preferred_element_type=jnp.float32
    ) + jnp.einsum("sid,sie->de", normed_low, key_low[:, 1], preferred_element_type=jnp.float32)
    grad_w_value = jnp.einsum(
        "sid,sie->de", mem_low, value_low[:, 0], preferred_element_type=jnp.float32
    ) + jnp.einsum("sid,sie->de", normed_low, value_low[:, 1], preferred_element_type=jnp.float32)
    grad_normed = grad_normed + jnp.einsum(
        "sie,de->sid", key_low[:, 1], w_key, preferred_element_type=jnp.float32
    )
    grad_normed = grad_normed + jnp.einsum(
        "sie,de->sid", value_low[:, 1], w_value, preferred_element_type=jnp.float32
    )
    grad_mem_normed = jnp.einsum(
        "sie,de->sid", key_low[:, 0], w_key, preferred_element_type=jnp.float32
    ) + jnp.einsum("sie,de->sid", value_low[:, 0], w_value, preferred_element_type=jnp.float32)
    unused_one, norm_one_back = jax.vjp(layer_norm, pooled, gain_one_f, shift_one_f)
    grad_pooled_norm, grad_gain_one, grad_shift_one = norm_one_back(grad_normed)
    unused_mem, norm_mem_back = jax.vjp(layer_norm, memory_f, gain_one_f, shift_one_f)
    unused_grad, grad_gain_mem, grad_shift_mem = norm_mem_back(grad_mem_normed)
    grad_gain_one = grad_gain_one + grad_gain_mem
    grad_shift_one = grad_shift_one + grad_shift_mem
    grad_pooled = grad_residual + grad_pooled_norm
    grad_sum = grad_pooled / own_lengths[:, :, None]
    grad_sum_all = lax.all_gather(grad_sum, "blk", axis=1, tiled=True)
    grad_chars = grad_f + jnp.take_along_axis(grad_sum_all, segment[:, :, None], axis=1)
    (
        grad_w_query,
        grad_w_key,
        grad_w_value,
        grad_w_rel,
        grad_w_out,
        grad_w_up,
        grad_w_down,
        grad_bias_u,
        grad_bias_v,
        grad_gain_one,
        grad_shift_one,
        grad_gain_two,
        grad_shift_two,
        grad_bias_up,
        grad_bias_down,
    ) = lax.psum(
        (
            grad_w_query,
            grad_w_key,
            grad_w_value,
            grad_w_rel,
            grad_w_out,
            grad_w_up,
            grad_w_down,
            grad_bias_u,
            grad_bias_v,
            grad_gain_one,
            grad_shift_one,
            grad_gain_two,
            grad_shift_two,
            grad_bias_up,
            grad_bias_down,
        ),
        ("seq", "blk"),
    )
    return (
        out_chars,
        grad_chars,
        new_memory,
        grad_w_query,
        grad_w_key,
        grad_w_value,
        grad_w_rel,
        grad_w_out,
        grad_w_up,
        grad_w_down,
        grad_bias_u,
        grad_bias_v,
        grad_gain_one,
        grad_shift_one,
        grad_gain_two,
        grad_shift_two,
        grad_bias_up,
        grad_bias_down,
    )


def solution(mesh):
    placed = (
        P("seq", "blk", None),
        P("seq", None),
        P("seq", "blk", None),
        P("seq", "blk", None),
        P(),
        P(),
        P(),
        P(),
        P(),
        P(),
        P(),
        P(),
        P(),
        P(),
        P(),
        P(),
        P(),
        P(),
        P(),
    )
    return jax.shard_map(
        shards_whole if fits_whole(mesh) else shards,
        mesh=mesh,
        in_specs=placed,
        out_specs=(
            P("seq", "blk", None),
            P("seq", "blk", None),
            P("seq", "blk", None),
            P(),
            P(),
            P(),
            P(),
            P(),
            P(),
            P(),
            P(),
            P(),
            P(),
            P(),
            P(),
            P(),
            P(),
            P(),
        ),
        check_vma=False,
    )
```

profile of v0, /device:TPU:0, one launch (start us, length us, event | category | flops | bytes accessed | tf_op | source)
XLA Modules:
  0.0 127.7 jit_solution(8643996959296766632)
XLA Ops:
  0.7 114.3 %layer.1 = (bf16[4,128,512]{2,1,0:T(8,128)(2,1)}, bf16[4,384,512]{2,1,0:T(8,128)(2,1)}, bf16[4,128,512]{2,1,0:T(8,128)(2,1)}, bf16[4,384,512]{2,1,0:T(8,128)(2,1...) custom-call(bf16[4,512,512]{2,1,0:T(8,128)(2,1)} %chars.3, s32[4,512]{1,0:T(4,128)} %lengths.3, ...), custom_call_target="tpu_custom_call" | custom-call | tf_op jit(solution)/shard_map/layer/pallas_call | solution.py:963
  115.0 12.6 %spread.1 = (bf16[4,512,512]{2,1,0:T(8,128)(2,1)}, f32[4,512,512]{2,1,0:T(8,128)}, bf16[4,128,512]{2,1,0:T(8,128)(2,1)}, f32[512,512]{1,0:T(8,128)}, f32[512,512...) custom-call(s32[4,512]{1,0:T(4,128)} %lengths.3, ...), custom_call_target="tpu_custom_call" | custom-call | tf_op jit(solution)/shard_map/spread/pallas_call | solution.py:997
where the time goes:
time: 128 us
  Pallas kernels  127 us (99%)
    pallas_call x1, Pallas kernels, shards_whole(): pl.pallas_call(functools.partial(layer_kernel, tuple(scratch)), out_shape...  114 us
    pallas_call x1, Pallas kernels, shards_whole(): pl.pallas_call(spread_kernel, grid=(count,), out_shape=[jax.ShapeDtypeStr...  12.6 us

commit v1 on v0

--- a/solution.py
+++ b/solution.py
@@ -170,10 +170,9 @@
 
     def add(self, k, n, start, size):
         span = rows_at(self.offset(k, n) + start, size)
-        self.g[span] = (self.g[span].astype(F32) + self.lands(k, n, start, size)[...].astype(F32)).astype(BF16)
+        self.g[span] = self.g[span] + self.lands(k, n, start, size)[...]
 
     def step(self, k, step):
-        g = self.g
         rows = PIECES[k][0]
         if step > 0:
             self.copies(step - 1, k).wait_send()
@@ -186,8 +185,8 @@
             self.add(k, step - 1, bit * half, half)
         elif step == 5:
             size = rows >> 5
-            total = g[rows_at(self.offset(k, 4), size)].astype(F32) + self.lands(k, 4)[...].astype(F32)
-            self.lands(k, 3, self.steps[k][3][1] * size, size)[...] = total.astype(BF16)
+            total = self.g[rows_at(self.offset(k, 4), size)] + self.lands(k, 4)[...]
+            self.lands(k, 3, self.steps[k][3][1] * size, size)[...] = total
             self.copies(step, k).start()
         elif step < STEPS - 1:
             self.copies(step, k).start()
@@ -434,7 +433,7 @@
 WEIGHTS = ("w_query", "w_key", "w_value", "w_rel", "w_out", "w_up", "w_down")
 
 
-def layer_scratch(seg, width, hidden):
+def layer_scratch(seg, width, hidden, shapes):
     def low(*shape):
         return pltpu.VMEM(shape, BF16)
 
@@ -484,6 +483,9 @@
         land_4=low(BASES[-1] >> 5, width),
         bias_up=full(1, hidden),
         vectors=full(16, width),
+        lengths=pltpu.VMEM((4, seg), jnp.int32),
+        **{f"raw_{name}": low(*shape) for name, shape in shapes.items()},
+        small_load=pltpu.SemaphoreType.DMA((len(VECTORS) + 1,)),
         small=full(16, width),
         small_sum=full(5, 16, width),
         small_land=full(5, 16, width),
@@ -757,47 +759,59 @@
     grads_rows = Rows(r, p, 1, grad_out, r.grad_inner, r.grads_quiet, r.grads_parts).back(
         r.grad_rows, grad_quiet, grad_loud
     )
+    raw = [getattr(r, f"raw_{name}") for name in VECTORS]
+    small_loads = [
+        pltpu.make_async_copy(src, dst, r.small_load.at[n])
+        for n, (src, dst) in enumerate(zip((*vectors, lengths), (*raw, r.lengths)))
+    ]
+    small_loads[-1].start()
     for n in range(4):
         chars_rows.load(n).start()
+    for copy in small_loads[:-1]:
+        copy.start()
     for n in range(4):
         grads_rows.load(n).start()
     for copy in loads:
         copy.start()
+    r.vec = lambda name: r.vectors[VECTORS.index(name) : VECTORS.index(name) + 1, :]
+
+    barrier = pltpu.get_barrier_semaphore()
+    others = [p.group(1), p.group(2), p.group(3), p.pair("y"), p.pair("near"), p.pair("far")]
+    for other in others:
+        pl.semaphore_signal(barrier, inc=1, device_id=other, device_id_type=MESH)
+    pl.semaphore_wait(barrier, len(others))
+
+    rows = memory.shape[1]
+
+    def memory_copy(k, slot):
+        to = (p.b + k) % 4
+        return remote(
+            memory.at[to], r.memory.at[rows_at(slot * rows, rows)], r.memory_send.at[k], r.memory_recv.at[slot], p.group(k)
+        )
+
+    own_memory = pltpu.make_async_copy(memory.at[p.b], r.memory.at[rows_at(p.b * rows, rows)], r.memory_send.at[0])
+    for k in (2, 3, 1):
+        memory_copy(k, p.b).start()
+    own_memory.start()
+    chars_rows.start_quiet()
+    small_loads[-1].wait()
+    ends, lens = span_columns(r.lengths[...], QUIET)
+    chars_rows.start_parts(ends, lens)
+    for copy in loads:
+        copy.wait()
+    for copy in small_loads[:-1]:
+        copy.wait()
     for n, name in enumerate(VECTORS):
-        value = vectors[n][...].astype(F32)
+        value = raw[n][...].astype(F32)
         if name == "bias_up":
             r.bias_up[...] = value.reshape(1, -1)
         elif value.ndim == 2:
             r.vectors[n : n + 1, :] = jnp.concatenate([value[h : h + 1, :] for h in range(value.shape[0])], axis=1)
         else:
             r.vectors[n : n + 1, :] = value.reshape(1, -1)
-    r.vec = lambda name: r.vectors[VECTORS.index(name) : VECTORS.index(name) + 1, :]
-
-    barrier = pltpu.get_barrier_semaphore()
-    others = [p.group(1), p.group(2), p.group(3), p.pair("y"), p.pair("near"), p.pair("far")]
-    for other in others:
-        pl.semaphore_signal(barrier, inc=1, device_id=other, device_id_type=MESH)
-    pl.semaphore_wait(barrier, len(others))
-
-    rows = memory.shape[1]
-
-    def memory_copy(k, slot):
-        to = (p.b + k) % 4
-        return remote(
-            memory.at[to], r.memory.at[rows_at(slot * rows, rows)], r.memory_send.at[k], r.memory_recv.at[slot], p.group(k)
-        )
-
-    own_memory = pltpu.make_async_copy(memory.at[p.b], r.memory.at[rows_at(p.b * rows, rows)], r.memory_send.at[0])
-    for k in (2, 3, 1):
-        memory_copy(k, p.b).start()
-    own_memory.start()
-    chars_rows.start_quiet()
-    ends, lens = span_columns(lengths[...], QUIET)
-    chars_rows.start_parts(ends, lens)
-    for copy in loads:
-        copy.wait()
     project_places(r)
-    chars_rows.join_parts()
+    waits = (1 - p.x) * p.c
+    pl.when(waits == 0)(chars_rows.join_parts)
     grads_rows.start_quiet()
     grads_rows.start_parts(ends, lens)
     own_memory.wait()
@@ -811,6 +825,8 @@
     def forward(block):
         project_segments(block, seg, r)
         attend(block, seg, r)
+        if block == 0:
+            pl.when(waits == 1)(chars_rows.join_parts)
         feed_forward_in(block, r)
 
     chars_rows.wait_quiet(0)
@@ -957,7 +973,8 @@
     seg, hidden = seg_lengths.shape[1], w_up.shape[1]
     rows = memory.shape[1]
     table = jnp.asarray(sine_table(2 * seg, width))
-    scratch = layer_scratch(seg, width, hidden)
+    vectors = (bias_u, bias_v, gain_one, shift_one, gain_two, shift_two, bias_up, bias_down)
+    scratch = layer_scratch(seg, width, hidden, {name: v.shape for name, v in zip(VECTORS, vectors)})
     anywhere, near = pl.BlockSpec(memory_space=pl.ANY), pl.BlockSpec(memory_space=pltpu.VMEM)
     loud = seg - QUIET
     kept, out_quiet, out_loud, grad_quiet, grad_loud, total, small = pl.pallas_call(
@@ -971,7 +988,7 @@
             jax.ShapeDtypeStruct((BASES[-1], width), BF16),
             jax.ShapeDtypeStruct((16, width), F32),
         ],
-        in_specs=[anywhere, near, anywhere, anywhere] + [near] * len(VECTORS) + [anywhere] * 8,
+        in_specs=[anywhere] * (12 + len(VECTORS)),
         out_specs=[anywhere] * 7,
         scratch_shapes=list(scratch.values()),
         compiler_params=pltpu.CompilerParams(
@@ -980,7 +997,7 @@
         name="layer",
     )(
         chars, seg_lengths, memory, grad_out,
-        bias_u, bias_v, gain_one, shift_one, gain_two, shift_two, bias_up, bias_down, table,
+        *vectors, table,
         w_query, w_key, w_value, w_rel, w_out, w_up, w_down,
     )
 

time: 128 us -> 126 us (0.984)
  Pallas kernels: 127 us -> 125 us
    pallas_call x1, Pallas kernels: 114 us -> 112 us  [shards_whole(): pl.pallas_call(functools.partial(layer_kernel, tuple(scratch)), out_shape...]
where the time goes in v1:
time: 126 us
  Pallas kernels  125 us (99%)
    pallas_call x1, Pallas kernels, shards_whole(): pl.pallas_call(functools.partial(layer_kernel, tuple(scratch)), out_shape...  112 us
    pallas_call x1, Pallas kernels, shards_whole(): pl.pallas_call(spread_kernel, grid=(count,), out_shape=[jax.ShapeDtypeStr...  12.6 us

profile of v1, /device:TPU:0, one launch (start us, length us, event | category | flops | bytes accessed | tf_op | source)
XLA Modules:
  0.0 125.8 jit_solution(10326071720272159885)
XLA Ops:
  0.7 112.3 %layer.1 = (bf16[4,128,512]{2,1,0:T(8,128)(2,1)}, bf16[4,384,512]{2,1,0:T(8,128)(2,1)}, bf16[4,128,512]{2,1,0:T(8,128)(2,1)}, bf16[4,384,512]{2,1,0:T(8,128)(2,1...) custom-call(bf16[4,512,512]{2,1,0:T(8,128)(2,1)} %chars.3, s32[4,512]{1,0:T(4,128)} %lengths.3, ...), custom_call_target="tpu_custom_call" | custom-call | tf_op jit(solution)/shard_map/layer/pallas_call | solution.py:980
  113.0 12.6 %spread.1 = (bf16[4,512,512]{2,1,0:T(8,128)(2,1)}, f32[4,512,512]{2,1,0:T(8,128)}, bf16[4,128,512]{2,1,0:T(8,128)(2,1)}, f32[512,512]{1,0:T(8,128)}, f32[512,512...) custom-call(s32[4,512]{1,0:T(4,128)} %lengths.3, ...), custom_call_target="tpu_custom_call" | custom-call | tf_op jit(solution)/shard_map/spread/pallas_call | solution.py:1014

commit v2 on v1

--- a/solution.py
+++ b/solution.py
@@ -45,38 +45,37 @@
 
 MESH = pl.DeviceIdType.MESH
 HALF = 256
-STEPS = 11
+FACTOR = dict(x=2, y=2, near=2, far=2, z=4, xy=4)
 AXES = ("x", "y", "near", "far")
 PIECES = tuple((1024, f"tile{n}") for n in range(4)) + ((512, "middle"),) + tuple((512, f"pair{n}") for n in range(4))
 BASES = tuple(sum(rows for rows, unused in PIECES[:n]) for n in range(len(PIECES) + 1))
 VECTORS = ("bias_u", "bias_v", "gain_one", "shift_one", "gain_two", "shift_two", "bias_up", "bias_down")
 ORDERS = (
-    (("y", "x", "near", "far"), ("x", "near", "y", "far")),
-    (("near", "y", "far", "x"), ("x", "y", "near", "far")),
-    (("near", "far", "y", "x"), ("y", "x", "near", "far")),
-    (("far", "y", "x", "near"), ("y", "x", "near", "far")),
-    (("y", "near", "x", "far"), ("x", "y", "far", "near")),
-    (("y", "x", "near", "far"), ("y", "near", "x", "far")),
-    (("near", "x", "y", "far"), ("x", "far", "y", "near")),
-    (("y", "x", "near", "far"), ("near", "y", "x", "far")),
-    (("y", "near", "x", "far"), ("near", "x", "y", "far")),
+    (("y", "near", "x", "far"), ("near", "y", "far", "x")),
+    (("far", "y", "x", "near"), ("near", "x", "y", "far")),
+    (("y", "x", "z"), ("x", "y", "z")),
+    (("x", "y", "z"), ("y", "x", "z")),
+    (("near", "far", "xy"), ("far", "near", "xy")),
+    (("y", "x", "near", "far"), ("far", "x", "y", "near")),
+    (("xy", "near", "far"), ("xy", "near", "far")),
+    (("y", "x", "z"), ("x", "y", "z")),
+    (("y", "x", "z"), ("y", "x", "z")),
 )
 DURING = (
-    ((0, 0),), ((1, 0),), ((2, 0),), ((0, 1), (3, 0)), ((1, 1),), ((2, 1), (3, 1), (4, 0)), ((0, 2),), (),
-    (), ((1, 2), (4, 1)), ((5, 0),), (), ((2, 2),), (), ((5, 1),), ((6, 0),), ((0, 3), (3, 2)), (),
-    ((1, 3), (6, 1)), ((4, 2),), ((7, 0), (2, 3)), (), ((5, 2),), ((0, 4), (7, 1)), ((1, 4), (3, 3)),
-    ((8, 0), (4, 3), (6, 2)), ((2, 4),),
+    ((0, 0),), ((1, 0),), ((2, 0),), ((3, 0), (0, 1)), (), ((1, 1), (2, 1), (4, 0)), ((3, 1),), (),
+    ((0, 2), (4, 1)), (), ((5, 0),), (), ((2, 2),), (), ((5, 1),), ((6, 0),), ((3, 2), (1, 2)), ((0, 3),),
+    ((6, 1),), ((2, 3),), ((7, 0),), ((4, 2),), ((3, 3), (5, 2)), ((1, 3), (7, 1)), ((0, 4),), ((8, 0),),
+    ((2, 4),),
 )
 AFTER = (
-    (8, 1), (0, 5), (7, 2), (5, 3), (1, 5), (3, 4), (4, 4), (6, 3), (2, 5), (8, 2), (7, 3), (5, 4), (0, 6),
-    (1, 6), (6, 4), (3, 5), (4, 5), (8, 3), (2, 6), (0, 7), (7, 4), (5, 5), (8, 4), (1, 7), (6, 5), (3, 6),
-    (4, 6), (2, 7), (0, 8), (7, 5), (5, 6), (8, 5), (6, 6), (3, 7), (1, 8), (4, 7), (2, 8), (7, 6), (0, 9),
-    (6, 7), (5, 7), (8, 6), (3, 8), (4, 8), (0, 10), (1, 9), (2, 9), (7, 7), (8, 7), (5, 8), (1, 10), (6, 8),
-    (2, 10), (4, 9), (7, 8), (3, 9), (8, 8), (4, 10), (5, 9), (6, 9), (3, 10), (7, 9), (5, 10), (8, 9),
-    (6, 10), (7, 10), (8, 10),
+    (6, 2), (8, 1), (5, 3), (4, 3), (1, 4), (7, 2), (3, 4), (6, 3), (8, 2), (0, 5), (5, 4), (2, 5), (1, 5),
+    (7, 3), (4, 4), (8, 3), (3, 5), (6, 4), (0, 6), (2, 6), (5, 5), (1, 6), (4, 5), (7, 4), (3, 6), (8, 4),
+    (6, 5), (0, 7), (5, 6), (2, 7), (1, 7), (4, 6), (6, 6), (2, 8), (7, 5), (3, 7), (0, 8), (8, 5), (5, 7),
+    (1, 8), (3, 8), (4, 7), (7, 6), (6, 7), (8, 6), (4, 8), (5, 8), (6, 8), (0, 9), (7, 7), (0, 10), (1, 9),
+    (7, 8), (8, 7), (5, 9), (1, 10), (8, 8), (5, 10),
 )
-BACK_DURING = (6, 8, 11, 13, 16, 21, 22, 24)
-BACK_AFTER = (10, 14, 20, 45, 49, 55, 56, 61)
+BACK_DURING = (10, 14)
+BACK_AFTER = (6, 40, 44, 45, 46, 46)
 
 
 class Place:
@@ -101,12 +100,35 @@
         turn = 1 - 2 * self.bit[axis]
         return reach[0] * turn, reach[1] * turn
 
-    def step(self, zero, one):
+    def peers(self, axis):
+        if axis == "z":
+            return self.z, [(self.line(j), (self.z + j) % 4, (self.z + 4 - j) % 4) for j in (1, 2, 3)]
+        if axis == "xy":
+            out = []
+            for across, along in ((1, 0), (0, 1), (1, 1)):
+                x, y = self.x + across * (1 - 2 * self.x), self.y + along * (1 - 2 * self.y)
+                device = (self.s + along * (1 - 2 * self.y), self.b + across * 2 * (1 - 2 * self.x))
+                out.append((device, x + 2 * y, x + 2 * y))
+            return self.x + 2 * self.y, out
+        bit = self.bit[axis]
+        return bit, [(self.pair(axis), 1 - bit, 1 - bit)]
+
+    def stage(self, zero, one):
         if zero == one:
-            return self.pair(zero), self.bit[zero]
-        away = [self.move(zero)[m] * (1 - self.c) + self.move(one)[m] * self.c for m in (0, 1)]
-        bit = self.bit[zero] * (1 - self.c) + self.bit[one] * self.c
-        return (self.s + away[0], self.b + away[1]), bit
+            return self.peers(zero)
+
+        def pick(a, b):
+            return a * (1 - self.c) + b * self.c
+
+        (own_zero, peers_zero), (own_one, peers_one) = self.peers(zero), self.peers(one)
+        peers = [
+            ((pick(d[0], e[0]), pick(d[1], e[1])), pick(i, j), pick(f, g))
+            for (d, i, f), (e, j, g) in zip(peers_zero, peers_one)
+        ]
+        return pick(own_zero, own_one), peers
+
+    def line(self, j):
+        return (((self.z + j) % 4) * 2 + self.y, self.b)
 
     def pair(self, axis):
         away = self.move(axis)
@@ -119,84 +141,123 @@
 
 def remote(src, dst, send, recv, to):
     return pltpu.make_async_remote_copy(src, dst, send, recv, device_id=to, device_id_type=MESH)
+
+
+def piece_rows(k):
+    rows = [PIECES[k][0] // 2]
+    for axis in ORDERS[k][0]:
+        rows.append(rows[-1] // FACTOR[axis])
+    return rows
+
+
+def piece_lands(k):
+    rows = piece_rows(k)
+    return [rows[0]] + [(FACTOR[axis] - 1) * rows[n + 1] for n, axis in enumerate(ORDERS[k][0])]
+
+
+LANDS = [[], 0]
+for _k in range(len(PIECES)):
+    LANDS[0].append([])
+    for _rows in piece_lands(_k):
+        LANDS[0][-1].append(LANDS[1])
+        LANDS[1] += _rows
 
 
 class Sum:
     def __init__(self, place, total, land, out, send, recv, store):
         self.p, self.g, self.land, self.out = place, total, land, out
         self.send, self.recv, self.store = send, recv, store
-        self.steps = [[place.step(*axes) for axes in zip(*orders)] for orders in ORDERS]
+        known = {}
+        self.stages = []
+        for orders in ORDERS:
+            for axes in zip(*orders):
+                if axes not in known:
+                    known[axes] = place.stage(*axes)
+            self.stages.append([known[axes] for axes in zip(*orders)])
 
     def offset(self, k, n):
-        start = BASES[k] + self.p.c * (PIECES[k][0] // 2)
+        rows = piece_rows(k)
+        start = BASES[k] + self.p.c * rows[0]
         for m in range(n):
-            start = start + self.steps[k][m][1] * (PIECES[k][0] >> (m + 2))
+            start = start + self.stages[k][m][0] * rows[m + 1]
         return start
 
-    def lands(self, k, n, start=0, size=None):
-        rows = PIECES[k][0] >> (n + 1)
-        return self.land[n].at[rows_at((BASES[k] >> (n + 1)) + start, rows if size is None else size)]
+    def lands(self, k, n, start, size):
+        return self.land.at[rows_at(LANDS[0][k][n] + start, size)]
 
     def copies(self, step, k, landing=False):
-        p, g = self.p, self.g
-        rows = PIECES[k][0]
-
-        def copy(src, dst, to):
-            return remote(src, dst, self.send.at[k], self.recv.at[k, step], to)
+        p, rows = self.p, piece_rows(k)
+        count = len(rows) - 1
+
+        def copy(src, dst, to, j=0):
+            return remote(src, dst, self.send.at[k, j], self.recv.at[k, step, j], to)
 
         if step == 0:
-            half = rows // 2
-            return copy(g.at[rows_at(BASES[k] + (1 - p.c) * half, half)], self.lands(k, 0), p.core())
-        if step <= 4:
-            to, bit = self.steps[k][step - 1]
-            size = rows >> (step + 1)
-            away = self.offset(k, step - 1) + (1 - bit) * size
-            return copy(g.at[rows_at(away, size)], self.lands(k, step), to)
-        if step <= 8:
-            n = 8 - step
-            to, bit = self.steps[k][n]
-            size = rows >> (n + 2)
-            dst = self.lands(k, n, (1 - bit if landing else bit) * size, size)
-            src = self.lands(k, 3, bit * size, size) if n == 3 else self.lands(k, n + 1)
-            return copy(src, dst, to)
-        half = rows // 2
-        span = BASES[k] + (1 - p.c if landing else p.c) * half
-        return copy(self.lands(k, 0), self.out.at[rows_at(span, half)], p.core())
+            src = self.g.at[rows_at(BASES[k] + (1 - p.c) * rows[0], rows[0])]
+            return [copy(src, self.lands(k, 0, 0, rows[0]), p.core())]
+        if step == 2 * count + 1:
+            span = BASES[k] + (1 - p.c if landing else p.c) * rows[0]
+            return [copy(self.lands(k, 0, 0, rows[0]), self.out.at[rows_at(span, rows[0])], p.core())]
+        n = step - 1 if step <= count else 2 * count - step
+        size = rows[n + 1]
+        own, peers = self.stages[k][n]
+        if step <= count:
+            start = self.offset(k, n)
+            return [
+                copy(self.g.at[rows_at(start + at * size, size)], self.lands(k, n + 1, j * size, size), to, j)
+                for j, (to, at, unused) in enumerate(peers)
+            ]
+        src = self.lands(k, n, own * size, size) if n == count - 1 else self.lands(k, n + 1, 0, size)
+        return [
+            copy(src, self.lands(k, n, (back if landing else own) * size, size), to, j)
+            for j, (to, unused, back) in enumerate(peers)
+        ]
 
     def own(self, k):
-        half = PIECES[k][0] // 2
-        span = rows_at(BASES[k] + self.p.c * half, half)
-        return pltpu.make_async_copy(self.lands(k, 0), self.out.at[span], self.store.at[k])
-
-    def add(self, k, n, start, size):
-        span = rows_at(self.offset(k, n) + start, size)
-        self.g[span] = self.g[span] + self.lands(k, n, start, size)[...]
+        rows = piece_rows(k)[0]
+        span = rows_at(BASES[k] + self.p.c * rows, rows)
+        return pltpu.make_async_copy(self.lands(k, 0, 0, rows), self.out.at[span], self.store.at[k])
+
+    def added(self, k, n, start, size):
+        mine = self.g[rows_at(self.offset(k, n) + start, size)]
+        if n == 0 or len(self.stages[k][n - 1][1]) == 1:
+            return mine + self.lands(k, n, start, size)[...]
+        whole = piece_rows(k)[n]
+        mine = mine.astype(F32)
+        for j in range(len(self.stages[k][n - 1][1])):
+            mine = mine + self.lands(k, n, j * whole + start, size)[...].astype(F32)
+        return mine.astype(BF16)
 
     def step(self, k, step):
-        rows = PIECES[k][0]
+        rows = piece_rows(k)
+        count = len(rows) - 1
         if step > 0:
-            self.copies(step - 1, k).wait_send()
-            self.copies(step - 1, k, landing=True).wait_recv()
-        if 1 <= step <= 4:
-            half = rows >> (step + 1)
-            bit = self.steps[k][step - 1][1]
-            self.add(k, step - 1, (1 - bit) * half, half)
-            self.copies(step, k).start()
-            self.add(k, step - 1, bit * half, half)
-        elif step == 5:
-            size = rows >> 5
-            total = self.g[rows_at(self.offset(k, 4), size)] + self.lands(k, 4)[...]
-            self.lands(k, 3, self.steps[k][3][1] * size, size)[...] = total
-            self.copies(step, k).start()
-        elif step < STEPS - 1:
-            self.copies(step, k).start()
-        if 6 <= step <= 8:
-            n = 8 - step
-            size = rows >> (n + 2)
-            self.lands(k, n, self.steps[k][n][1] * size, size)[...] = self.lands(k, n + 1)[...]
-        if step == STEPS - 2:
+            for copy in self.copies(step - 1, k):
+                copy.wait_send()
+            for copy in self.copies(step - 1, k, landing=True):
+                copy.wait_recv()
+        if 1 <= step <= count:
+            n, size = step - 1, rows[step]
+            own, peers = self.stages[k][n]
+            copies = self.copies(step, k)
+            for index, copy in zip([at for unused, at, other in peers] + [own], copies + [None]):
+                part = self.added(k, n, index * size, size)
+                self.g[rows_at(self.offset(k, n) + index * size, size)] = part
+                if copy is not None:
+                    copy.start()
+        elif step <= 2 * count + 1:
+            if step == count + 1:
+                size = rows[count]
+                self.lands(k, count - 1, self.stages[k][count - 1][0] * size, size)[...] = self.added(k, count, 0, size)
+            for copy in self.copies(step, k):
+                copy.start()
+        if count + 2 <= step <= 2 * count:
+            n = 2 * count - step
+            size = rows[n + 1]
+            self.lands(k, n, self.stages[k][n][0] * size, size)[...] = self.lands(k, n + 1, 0, size)[...]
+        if step == 2 * count + 1:
             self.own(k).start()
-        if step == STEPS - 1:
+        if step == 2 * count + 2:
             self.own(k).wait()
 
 
@@ -363,6 +424,12 @@
         r.slope[rows, cols] = slope.astype(BF16)
 
 
+def feed_forward_out(n, r):
+    rows = slice(n * HALF, (n + 1) * HALF)
+    branch = mm(r.hidden[rows], r.w_down[...]) + r.vec("bias_down")
+    r.out_rows[rows] = (r.residual[rows] + branch).astype(BF16)
+
+
 def feed_forward_back(n, r):
     cols = slice(n * 512, (n + 1) * 512)
     r.total[rows_at(BASES[n], 512)] = mm(r.grad_down_t[...], r.hidden[:, cols]).astype(BF16)
@@ -407,7 +474,8 @@
 
 
 QUIET = 384
-BACK_PARTS = 8
+BACK_PARTS = 6
+BACK_EARLY = BACK_PARTS * HALF // QUIET
 KEPT_DURING = (18, 9, 14)
 
 
@@ -476,11 +544,7 @@
         grads_quiet=low(QUIET, width),
         grads_parts=low(7, seg - QUIET, width),
         total=low(BASES[-1], width),
-        land_0=low(BASES[-1] >> 1, width),
-        land_1=low(BASES[-1] >> 2, width),
-        land_2=low(BASES[-1] >> 3, width),
-        land_3=low(BASES[-1] >> 4, width),
-        land_4=low(BASES[-1] >> 5, width),
+        land=low(LANDS[1], width),
         bias_up=full(1, hidden),
         vectors=full(16, width),
         lengths=pltpu.VMEM((4, seg), jnp.int32),
@@ -501,8 +565,8 @@
         kept_recv=pltpu.SemaphoreType.DMA((4,)),
         back_send=pltpu.SemaphoreType.DMA((2, 5)),
         back_recv=pltpu.SemaphoreType.DMA((2, 2, 4)),
-        sum_send=pltpu.SemaphoreType.DMA((len(PIECES),)),
-        sum_recv=pltpu.SemaphoreType.DMA((len(PIECES), STEPS - 1)),
+        sum_send=pltpu.SemaphoreType.DMA((len(PIECES), 3)),
+        sum_recv=pltpu.SemaphoreType.DMA((len(PIECES), 10, 3)),
         small_send=pltpu.SemaphoreType.DMA((5,)),
         small_recv=pltpu.SemaphoreType.DMA((5,)),
         small_sem=pltpu.SemaphoreType.DMA,
@@ -776,7 +840,7 @@
     r.vec = lambda name: r.vectors[VECTORS.index(name) : VECTORS.index(name) + 1, :]
 
     barrier = pltpu.get_barrier_semaphore()
-    others = [p.group(1), p.group(2), p.group(3), p.pair("y"), p.pair("near"), p.pair("far")]
+    others = [p.group(1), p.group(2), p.group(3), *(to for to, unused, other in p.peers("xy")[1][1:]), p.line(1), p.line(2), p.line(3)]
     for other in others:
         pl.semaphore_signal(barrier, inc=1, device_id=other, device_id_type=MESH)
     pl.semaphore_wait(barrier, len(others))
@@ -833,6 +897,9 @@
     r.pooled[0:HALF] = chars_rows.quiet[0:HALF].astype(F32)
     forward(0)
     grads_rows.join_parts()
+    feed_forward_out(0, r)
+    for part in range(BACK_EARLY):
+        chars_rows.start_quiet_back(part)
     chars_rows.wait_quiet(1)
     r.pooled[HALF:QUIET] = chars_rows.quiet[HALF:QUIET].astype(F32)
     r.pooled[QUIET:seg] = chars_rows.wait_parts() / own_lens
@@ -850,8 +917,7 @@
     r.small[...] = jnp.zeros(r.small.shape, F32)
     r.small[6:7, :] = jnp.sum(low.astype(F32), axis=0, keepdims=True)
 
-    land = [getattr(r, f"land_{n}") for n in range(5)]
-    sums = Sum(p, r.total, land, total_out, r.sum_send, r.sum_recv, r.store_sem)
+    sums = Sum(p, r.total, r.land, total_out, r.sum_send, r.sum_recv, r.store_sem)
 
     rows_kept = Kept(r, p, chars, kept)
 
@@ -863,7 +929,7 @@
                 rows_kept.start_late(to)
         for part, at in enumerate(BACK_DURING):
             if at == n:
-                chars_rows.start_quiet_back(part)
+                chars_rows.start_quiet_back(BACK_EARLY + part)
         for k, step in DURING[n]:
             sums.step(k, step)
 
@@ -876,7 +942,7 @@
     for n in range(4):
         feed_forward_back(n, r)
         take(n)
-    r.out_rows[...] = (r.residual[...] + (mm(r.hidden[...], r.w_down[...]) + r.vec("bias_down"))).astype(BF16)
+    feed_forward_out(1, r)
     chars_rows.start_back()
     take(4)
     middle_back(r, BASES[4])

time: 126 us -> 124 us (0.984)
  Pallas kernels: 125 us -> 123 us
    pallas_call x1, Pallas kernels: 112 us -> 110 us  [shards_whole(): pl.pallas_call(functools.partial(layer_kernel, tuple(scratch)), out_shape...]
where the time goes in v2:
time: 124 us
  Pallas kernels  123 us (99%)
    pallas_call x1, Pallas kernels, shards_whole(): pl.pallas_call(functools.partial(layer_kernel, tuple(scratch)), out_shape...  110 us
    pallas_call x1, Pallas kernels, shards_whole(): pl.pallas_call(spread_kernel, grid=(count,), out_shape=[jax.ShapeDtypeStr...  12.6 us

profile of v2, /device:TPU:0, one launch (start us, length us, event | category | flops | bytes accessed | tf_op | source)
XLA Modules:
  0.0 123.9 jit_solution(13675964823375284366)
XLA Ops:
  0.7 110.5 %layer.1 = (bf16[4,128,512]{2,1,0:T(8,128)(2,1)}, bf16[4,384,512]{2,1,0:T(8,128)(2,1)}, bf16[4,128,512]{2,1,0:T(8,128)(2,1)}, bf16[4,384,512]{2,1,0:T(8,128)(2,1...) custom-call(bf16[4,512,512]{2,1,0:T(8,128)(2,1)} %chars.3, s32[4,512]{1,0:T(4,128)} %lengths.3, ...), custom_call_target="tpu_custom_call" | custom-call | tf_op jit(solution)/shard_map/layer/pallas_call | solution.py:1046
  111.2 12.6 %spread.1 = (bf16[4,512,512]{2,1,0:T(8,128)(2,1)}, f32[4,512,512]{2,1,0:T(8,128)}, bf16[4,128,512]{2,1,0:T(8,128)(2,1)}, f32[512,512]{1,0:T(8,128)}, f32[512,512...) custom-call(s32[4,512]{1,0:T(4,128)} %lengths.3, ...), custom_call_target="tpu_custom_call" | custom-call | tf_op jit(solution)/shard_map/spread/pallas_call | solution.py:1080

commit v3 on v2

--- a/solution.py
+++ b/solution.py
@@ -155,12 +155,24 @@
     return [rows[0]] + [(FACTOR[axis] - 1) * rows[n + 1] for n, axis in enumerate(ORDERS[k][0])]
 
 
-LANDS = [[], 0]
-for _k in range(len(PIECES)):
-    LANDS[0].append([])
-    for _rows in piece_lands(_k):
-        LANDS[0][-1].append(LANDS[1])
-        LANDS[1] += _rows
+def piece_peers(k):
+    stages = [FACTOR[axis] - 1 for axis in ORDERS[k][0]]
+    return [1, *stages, *stages[::-1], 1]
+
+
+def starts(counts):
+    out, end = [], 0
+    for piece in counts:
+        out.append([])
+        for count in piece:
+            out[-1].append(end)
+            end += count
+    return out, end
+
+
+LANDS = starts([piece_lands(k) for k in range(len(PIECES))])
+SENDS = starts([[max(piece_peers(k))] for k in range(len(PIECES))])
+RECVS = starts([piece_peers(k) for k in range(len(PIECES))])
 
 
 class Sum:
@@ -190,7 +202,7 @@
         count = len(rows) - 1
 
         def copy(src, dst, to, j=0):
-            return remote(src, dst, self.send.at[k, j], self.recv.at[k, step, j], to)
+            return remote(src, dst, self.send.at[SENDS[0][k][0] + j], self.recv.at[RECVS[0][k][step] + j], to)
 
         if step == 0:
             src = self.g.at[rows_at(BASES[k] + (1 - p.c) * rows[0], rows[0])]
@@ -474,6 +486,7 @@
 
 
 QUIET = 384
+MOST = 16
 BACK_PARTS = 6
 BACK_EARLY = BACK_PARTS * HALF // QUIET
 KEPT_DURING = (18, 9, 14)
@@ -565,8 +578,8 @@
         kept_recv=pltpu.SemaphoreType.DMA((4,)),
         back_send=pltpu.SemaphoreType.DMA((2, 5)),
         back_recv=pltpu.SemaphoreType.DMA((2, 2, 4)),
-        sum_send=pltpu.SemaphoreType.DMA((len(PIECES), 3)),
-        sum_recv=pltpu.SemaphoreType.DMA((len(PIECES), 10, 3)),
+        sum_send=pltpu.SemaphoreType.DMA((SENDS[1],)),
+        sum_recv=pltpu.SemaphoreType.DMA((RECVS[1],)),
         small_send=pltpu.SemaphoreType.DMA((5,)),
         small_recv=pltpu.SemaphoreType.DMA((5,)),
         small_sem=pltpu.SemaphoreType.DMA,
@@ -574,10 +587,18 @@
     )
 
 
+def chip_spans(places, loud):
+    half = 2 * places
+    most = -(-(loud - half // MOST) // 16) * 16
+    least = (half - QUIET) // MOST // 16 * 16
+    return (0, most), (least, loud - least)
+
+
 class Rows:
     def __init__(self, r, place, way, source, stage, quiet, parts):
         self.r, self.p, self.way = r, place, way
         self.source, self.stage, self.quiet, self.parts = source, stage, quiet, parts
+        self.spans = [pl.ds(*span) for span in chip_spans(source.shape[1], parts.shape[1])]
 
     def load(self, n):
         cols = pl.ds(pl.multiple_of(n * 512, 512), 512)
@@ -607,15 +628,23 @@
         def _():
             self.quiet_copy(1, part).wait_recv()
 
-    def parts_copy(self, n):
+    def on_chip(self, act):
+        for chip in range(2):
+            pl.when(self.p.x == chip)(functools.partial(act, chip))
+
+    def parts_copy(self, n, chip=None):
         src, dst, to = ((3, 1, self.p.core()), (4, 5, self.p.core()), (6, 2, self.p.across()))[n]
+        span = pl.ds(0, self.parts.shape[1]) if chip is None else self.spans[chip]
         return remote(
-            self.parts.at[src],
-            self.parts.at[dst],
+            self.parts.at[src, span],
+            self.parts.at[dst, span],
             self.r.parts_send.at[self.way, n],
             self.r.parts_recv.at[self.way, n],
             to,
         )
+
+    def clear(self):
+        self.parts[2] = jnp.zeros(self.parts.shape[1:], BF16)
 
     def part(self, to, ends, lens):
         self.load(to).wait()
@@ -635,16 +664,17 @@
     def join_parts(self):
         self.parts_copy(1).wait_recv()
         self.parts[6] = (self.parts[6].astype(F32) + self.parts[5].astype(F32)).astype(BF16)
-        self.parts_copy(2).start()
+        self.on_chip(lambda chip: self.parts_copy(2, chip).start())
 
     def wait_parts(self):
         self.parts_copy(0).wait_recv()
-        self.parts_copy(2).wait_recv()
+        self.on_chip(lambda chip: self.parts_copy(2, 1 - chip).wait_recv())
         return sum(self.parts[n].astype(F32) for n in range(3))
 
     def wait_sent(self):
-        for n in range(3):
+        for n in range(2):
             self.parts_copy(n).wait_send()
+        self.on_chip(lambda chip: self.parts_copy(2, chip).wait_send())
 
         @pl.when(self.p.b == 0)
         def _():
@@ -656,17 +686,20 @@
         self.rows, self.quiet_out, self.loud_out = rows, quiet_out, loud_out
         return self
 
-    def loud_rows(self):
-        return self.rows.at[pl.ds(QUIET, self.rows.shape[0] - QUIET)]
+    def loud_rows(self, chip):
+        start, size = chip_spans(self.source.shape[1], self.parts.shape[1])[chip]
+        return self.rows.at[pl.ds(QUIET + start, size)]
 
     def quiet_rows(self):
         return self.rows.at[pl.ds(0, QUIET)]
 
-    def loud_copy(self, n, slot):
+    def loud_copy(self, n, slot, chip):
         r, p, way = self.r, self.p, self.way
-        src = self.loud_out.at[slot] if n == 2 else self.loud_rows()
+        dst = self.loud_out.at[slot, self.spans[chip]]
         to = p.across() if n == 1 else p.core()
-        return remote(src, self.loud_out.at[slot], r.back_send.at[way, n], r.back_recv.at[way, 0, slot], to)
+        return remote(
+            dst if n == 2 else self.loud_rows(chip), dst, r.back_send.at[way, n], r.back_recv.at[way, 0, slot], to
+        )
 
     def quiet_back(self, slot, start=0, size=QUIET):
         r, way = self.r, self.way
@@ -679,19 +712,21 @@
             (self.p.s, 0),
         )
 
-    def own_copies(self):
-        r, p, way = self.r, self.p, self.way
-        loud = pltpu.make_async_copy(self.loud_rows(), self.loud_out.at[p.b], r.back_send.at[way, 4])
-        quiet = pltpu.make_async_copy(self.quiet_rows(), self.quiet_out.at[0], r.back_send.at[way, 3])
-        return loud, quiet
+    def own_quiet(self):
+        return pltpu.make_async_copy(self.quiet_rows(), self.quiet_out.at[0], self.r.back_send.at[self.way, 3])
+
+    def own_loud(self, chip):
+        dst = self.loud_out.at[self.p.b, self.spans[chip]]
+        return pltpu.make_async_copy(self.loud_rows(chip), dst, self.r.back_send.at[self.way, 4])
 
     def start_back(self):
-        p = self.p
-        loud, quiet = self.own_copies()
-        self.loud_copy(1, p.b).start()
-        self.loud_copy(0, p.b).start()
-        pl.when(p.b == 0)(quiet.start)
-        loud.start()
+        def start(chip):
+            self.loud_copy(1, self.p.b, 1 - chip).start()
+            self.loud_copy(0, self.p.b, chip).start()
+            self.own_loud(chip).start()
+
+        self.on_chip(start)
+        pl.when(self.p.b == 0)(self.own_quiet().start)
 
     def start_quiet_back(self, n):
         size = QUIET // BACK_PARTS
@@ -699,24 +734,31 @@
 
     def pass_on(self):
         away = self.p.across()[1]
-        self.loud_copy(1, away).wait_recv()
-        self.loud_copy(2, away).start()
+
+        def pass_on(chip):
+            self.loud_copy(1, away, chip).wait_recv()
+            self.loud_copy(2, away, chip).start()
+
+        self.on_chip(pass_on)
 
     def wait_back(self):
         p = self.p
         sibling, away = p.core()[1], p.across()[1]
-        loud, quiet = self.own_copies()
-        for n in (0, 1):
-            self.loud_copy(n, p.b).wait_send()
-        self.loud_copy(2, away).wait_send()
-        loud.wait()
+
+        def wait(chip):
+            self.loud_copy(0, p.b, chip).wait_send()
+            self.loud_copy(1, p.b, 1 - chip).wait_send()
+            self.loud_copy(2, away, chip).wait_send()
+            self.own_loud(chip).wait()
+            self.loud_copy(0, sibling, chip).wait_recv()
+            self.loud_copy(2, away + sibling - p.b, chip).wait_recv()
+
+        self.on_chip(wait)
         pl.when(p.b != 0)(self.quiet_back(p.b).wait_send)
-        pl.when(p.b == 0)(quiet.wait)
-        self.loud_copy(0, sibling).wait_recv()
-        self.loud_copy(2, away + sibling - p.b).wait_recv()
 
         @pl.when(p.b == 0)
         def _():
+            self.own_quiet().wait()
             for n in (1, 2, 3):
                 self.quiet_back(n).wait_recv()
 
@@ -839,6 +881,8 @@
         copy.start()
     r.vec = lambda name: r.vectors[VECTORS.index(name) : VECTORS.index(name) + 1, :]
 
+    chars_rows.clear()
+    grads_rows.clear()
     barrier = pltpu.get_barrier_semaphore()
     others = [p.group(1), p.group(2), p.group(3), *(to for to, unused, other in p.peers("xy")[1][1:]), p.line(1), p.line(2), p.line(3)]
     for other in others:
@@ -1009,12 +1053,16 @@
     place = (ramp((places, seg - QUIET), 0) + b * places).astype(F32)
     chosen = jnp.where((place < end) & (place >= end - length), 1.0, 0.0).astype(BF16)
     first = b == 0
+    spans = chip_spans(places, seg - QUIET)
+    here = ramp((seg - QUIET, 1), 0)
+    inside = [(here >= start) & (here < start + size) for start, size in spans]
+    there = jnp.where(b < 2, inside[0].astype(F32), inside[1].astype(F32)) > 0
     kept[...] = rows[...]
     for source, quiet, loud, out in (
         (chars, out_quiet, out_loud, out_chars),
         (grad_out, grad_quiet, grad_loud, grad_chars),
     ):
-        spread = mm(chosen, loud[0])
+        spread = mm(chosen, jnp.where(there, loud[0].astype(F32), 0.0).astype(BF16))
         whole = source[0].astype(F32) + spread
         out[0, QUIET:places] = whole[QUIET:].astype(out.dtype)
         out[0, 0:QUIET] = (whole[:QUIET] + jnp.where(first, quiet[0].astype(F32), 0.0)).astype(out.dtype)

time: 124 us -> 118 us (0.952)
  Pallas kernels: 123 us -> 117 us
    pallas_call x1, Pallas kernels: 110 us -> 104 us  [shards_whole(): pl.pallas_call(functools.partial(layer_kernel, tuple(scratch)), out_shape...]
where the time goes in v3:
time: 118 us
  Pallas kernels  117 us (99%)
    pallas_call x1, Pallas kernels, shards_whole(): pl.pallas_call(functools.partial(layer_kernel, tuple(scratch)), out_shape...  104 us
    pallas_call x1, Pallas kernels, shards_whole(): pl.pallas_call(spread_kernel, grid=(count,), out_shape=[jax.ShapeDtypeStr...  12.6 us

profile of v3, /device:TPU:0, one launch (start us, length us, event | category | flops | bytes accessed | tf_op | source)
XLA Modules:
  0.0 117.9 jit_solution(5154839448661097429)
XLA Ops:
  0.7 104.4 %layer.1 = (bf16[4,128,512]{2,1,0:T(8,128)(2,1)}, bf16[4,384,512]{2,1,0:T(8,128)(2,1)}, bf16[4,128,512]{2,1,0:T(8,128)(2,1)}, bf16[4,384,512]{2,1,0:T(8,128)(2,1...) custom-call(bf16[4,512,512]{2,1,0:T(8,128)(2,1)} %chars.3, s32[4,512]{1,0:T(4,128)} %lengths.3, ...), custom_call_target="tpu_custom_call" | custom-call | tf_op jit(solution)/shard_map/layer/pallas_call | solution.py:1094
  105.1 12.6 %spread.1 = (bf16[4,512,512]{2,1,0:T(8,128)(2,1)}, f32[4,512,512]{2,1,0:T(8,128)}, bf16[4,128,512]{2,1,0:T(8,128)(2,1)}, f32[512,512]{1,0:T(8,128)}, f32[512,512...) custom-call(s32[4,512]{1,0:T(4,128)} %lengths.3, ...), custom_call_target="tpu_custom_call" | custom-call | tf_op jit(solution)/shard_map/spread/pallas_call | solution.py:1128

commit v4 on v3

--- a/solution.py
+++ b/solution.py
@@ -51,31 +51,31 @@
 BASES = tuple(sum(rows for rows, unused in PIECES[:n]) for n in range(len(PIECES) + 1))
 VECTORS = ("bias_u", "bias_v", "gain_one", "shift_one", "gain_two", "shift_two", "bias_up", "bias_down")
 ORDERS = (
-    (("y", "near", "x", "far"), ("near", "y", "far", "x")),
-    (("far", "y", "x", "near"), ("near", "x", "y", "far")),
     (("y", "x", "z"), ("x", "y", "z")),
     (("x", "y", "z"), ("y", "x", "z")),
+    (("near", "y", "x", "far"), ("far", "x", "near", "y")),
+    (("y", "x", "near", "far"), ("near", "y", "x", "far")),
     (("near", "far", "xy"), ("far", "near", "xy")),
-    (("y", "x", "near", "far"), ("far", "x", "y", "near")),
-    (("xy", "near", "far"), ("xy", "near", "far")),
+    (("y", "x", "near", "far"), ("y", "x", "near", "far")),
     (("y", "x", "z"), ("x", "y", "z")),
+    (("x", "y", "z"), ("x", "y", "z")),
     (("y", "x", "z"), ("y", "x", "z")),
 )
 DURING = (
-    ((0, 0),), ((1, 0),), ((2, 0),), ((3, 0), (0, 1)), (), ((1, 1), (2, 1), (4, 0)), ((3, 1),), (),
-    ((0, 2), (4, 1)), (), ((5, 0),), (), ((2, 2),), (), ((5, 1),), ((6, 0),), ((3, 2), (1, 2)), ((0, 3),),
-    ((6, 1),), ((2, 3),), ((7, 0),), ((4, 2),), ((3, 3), (5, 2)), ((1, 3), (7, 1)), ((0, 4),), ((8, 0),),
-    ((2, 4),),
+    ((0, 0),), ((1, 0),), ((2, 0),), ((3, 0),), ((0, 1),), ((2, 1), (1, 1), (4, 0)), ((3, 1),), (), (),
+    ((4, 1),), ((0, 2), (5, 0)), (), (), ((1, 2),), ((5, 1),), ((6, 0),), ((2, 2),), ((0, 3),), (),
+    ((6, 1), (3, 2)), ((1, 3), (7, 0)), (), ((5, 2), (4, 2)), ((2, 3), (7, 1)), (), ((0, 4), (6, 2), (8, 0)),
+    ((5, 3), (3, 3)),
 )
 AFTER = (
-    (6, 2), (8, 1), (5, 3), (4, 3), (1, 4), (7, 2), (3, 4), (6, 3), (8, 2), (0, 5), (5, 4), (2, 5), (1, 5),
-    (7, 3), (4, 4), (8, 3), (3, 5), (6, 4), (0, 6), (2, 6), (5, 5), (1, 6), (4, 5), (7, 4), (3, 6), (8, 4),
-    (6, 5), (0, 7), (5, 6), (2, 7), (1, 7), (4, 6), (6, 6), (2, 8), (7, 5), (3, 7), (0, 8), (8, 5), (5, 7),
-    (1, 8), (3, 8), (4, 7), (7, 6), (6, 7), (8, 6), (4, 8), (5, 8), (6, 8), (0, 9), (7, 7), (0, 10), (1, 9),
-    (7, 8), (8, 7), (5, 9), (1, 10), (8, 8), (5, 10),
+    (2, 4), (1, 4), (8, 1), (4, 3), (7, 2), (6, 3), (5, 4), (3, 4), (0, 5), (2, 5), (8, 2), (1, 5), (7, 3),
+    (4, 4), (6, 4), (5, 5), (0, 6), (8, 3), (3, 5), (2, 6), (1, 6), (4, 5), (7, 4), (6, 5), (5, 6), (0, 7),
+    (2, 7), (8, 4), (3, 6), (0, 8), (1, 7), (5, 7), (4, 6), (6, 6), (2, 8), (7, 5), (3, 7), (1, 8), (8, 5),
+    (5, 8), (6, 7), (7, 6), (4, 7), (6, 8), (3, 8), (4, 8), (8, 6), (5, 9), (2, 9), (5, 10), (7, 7), (3, 9),
+    (2, 10), (7, 8), (8, 7), (3, 10), (8, 8),
 )
-BACK_DURING = (10, 14)
-BACK_AFTER = (6, 40, 44, 45, 46, 46)
+BACK_DURING = (8, 13)
+BACK_AFTER = (0, 37, 43, 46, 51, 51)
 
 
 class Place:

time: 118 us -> 117 us (level)
    pallas_call x1, Pallas kernels: 104 us -> 103 us  [shards_whole(): pl.pallas_call(functools.partial(layer_kernel, tuple(scratch)), out_shape...]
where the time goes in v4:
time: 117 us; the launch traced here: 116 us
  Pallas kernels  116 us (99%)
    pallas_call x1, Pallas kernels, shards_whole(): pl.pallas_call(functools.partial(layer_kernel, tuple(scratch)), out_shape...  103 us
    pallas_call x1, Pallas kernels, shards_whole(): pl.pallas_call(spread_kernel, grid=(count,), out_shape=[jax.ShapeDtypeStr...  12.6 us

profile of v4, /device:TPU:0, one launch (start us, length us, event | category | flops | bytes accessed | tf_op | source)
XLA Modules:
  0.0 116.4 jit_solution(7517001545679511731)
XLA Ops:
  0.7 102.9 %layer.1 = (bf16[4,128,512]{2,1,0:T(8,128)(2,1)}, bf16[4,384,512]{2,1,0:T(8,128)(2,1)}, bf16[4,128,512]{2,1,0:T(8,128)(2,1)}, bf16[4,384,512]{2,1,0:T(8,128)(2,1...) custom-call(bf16[4,512,512]{2,1,0:T(8,128)(2,1)} %chars.3, s32[4,512]{1,0:T(4,128)} %lengths.3, ...), custom_call_target="tpu_custom_call" | custom-call | tf_op jit(solution)/shard_map/layer/pallas_call | solution.py:1094
  103.6 12.6 %spread.1 = (bf16[4,512,512]{2,1,0:T(8,128)(2,1)}, f32[4,512,512]{2,1,0:T(8,128)}, bf16[4,128,512]{2,1,0:T(8,128)(2,1)}, f32[512,512]{1,0:T(8,128)}, f32[512,512...) custom-call(s32[4,512]{1,0:T(4,128)} %lengths.3, ...), custom_call_target="tpu_custom_call" | custom-call | tf_op jit(solution)/shard_map/spread/pallas_call | solution.py:1128

commit v5 on v4

--- a/solution.py
+++ b/solution.py
@@ -562,12 +562,10 @@
         vectors=full(16, width),
         lengths=pltpu.VMEM((4, seg), jnp.int32),
         **{f"raw_{name}": low(*shape) for name, shape in shapes.items()},
-        small_load=pltpu.SemaphoreType.DMA((len(VECTORS) + 1,)),
         small=full(16, width),
         small_sum=full(5, 16, width),
         small_land=full(5, 16, width),
-        load_sem=pltpu.SemaphoreType.DMA((len(WEIGHTS) + 1,)),
-        stage_sem=pltpu.SemaphoreType.DMA((2, 4)),
+        local_sem=pltpu.SemaphoreType.DMA((max(8 + len(WEIGHTS) + 1 + len(VECTORS) + 1, SENDS[1]),)),
         memory_send=pltpu.SemaphoreType.DMA((4,)),
         memory_recv=pltpu.SemaphoreType.DMA((4,)),
         quiet_send=pltpu.SemaphoreType.DMA((2, 4, 2)),
@@ -578,7 +576,6 @@
         kept_recv=pltpu.SemaphoreType.DMA((4,)),
         back_send=pltpu.SemaphoreType.DMA((2, 5)),
         back_recv=pltpu.SemaphoreType.DMA((2, 2, 4)),
-        sum_send=pltpu.SemaphoreType.DMA((SENDS[1],)),
         sum_recv=pltpu.SemaphoreType.DMA((RECVS[1],)),
         small_send=pltpu.SemaphoreType.DMA((5,)),
         small_recv=pltpu.SemaphoreType.DMA((5,)),
@@ -602,7 +599,7 @@
 
     def load(self, n):
         cols = pl.ds(pl.multiple_of(n * 512, 512), 512)
-        return pltpu.make_async_copy(self.source.at[n], self.stage.at[:, cols], self.r.stage_sem.at[self.way, n])
+        return pltpu.make_async_copy(self.source.at[n], self.stage.at[:, cols], self.r.local_sem.at[self.way * 4 + n])
 
     def quiet_copy(self, to, part):
         r = self.r
@@ -856,7 +853,7 @@
     r.grad_key_t, r.grad_value_t = r.hidden.at[:, : 2 * seg], r.hidden.at[:, 2 * seg :]
     r.grad_place_t, r.grad_query = r.grad_inner.at[:, : 2 * seg], r.grad_inner.at[:, 2 * seg : 3 * seg]
     loads = [
-        pltpu.make_async_copy(src, dst, r.load_sem.at[n])
+        pltpu.make_async_copy(src, dst, r.local_sem.at[8 + n])
         for n, (src, dst) in enumerate(
             zip((*weights, table), [getattr(r, name) for name in WEIGHTS] + [r.table])
         )
@@ -867,7 +864,7 @@
     )
     raw = [getattr(r, f"raw_{name}") for name in VECTORS]
     small_loads = [
-        pltpu.make_async_copy(src, dst, r.small_load.at[n])
+        pltpu.make_async_copy(src, dst, r.local_sem.at[8 + len(WEIGHTS) + 1 + n])
         for n, (src, dst) in enumerate(zip((*vectors, lengths), (*raw, r.lengths)))
     ]
     small_loads[-1].start()
@@ -961,7 +958,7 @@
     r.small[...] = jnp.zeros(r.small.shape, F32)
     r.small[6:7, :] = jnp.sum(low.astype(F32), axis=0, keepdims=True)
 
-    sums = Sum(p, r.total, r.land, total_out, r.sum_send, r.sum_recv, r.store_sem)
+    sums = Sum(p, r.total, r.land, total_out, r.local_sem, r.sum_recv, r.store_sem)
 
     rows_kept = Kept(r, p, chars, kept)
 

time: 117 us -> 116 us (level)
  no operation moved by 1% of the time
where the time goes in v5:
time: 116 us
  Pallas kernels  115 us (99%)
    pallas_call x1, Pallas kernels, shards_whole(): pl.pallas_call(functools.partial(layer_kernel, tuple(scratch)), out_shape...  103 us
    pallas_call x1, Pallas kernels, shards_whole(): pl.pallas_call(spread_kernel, grid=(count,), out_shape=[jax.ShapeDtypeStr...  12.6 us

profile of v5, /device:TPU:0, one launch (start us, length us, event | category | flops | bytes accessed | tf_op | source)
XLA Modules:
  0.0 116.1 jit_solution(8188917890086620497)
XLA Ops:
  0.7 102.7 %layer.1 = (bf16[4,128,512]{2,1,0:T(8,128)(2,1)}, bf16[4,384,512]{2,1,0:T(8,128)(2,1)}, bf16[4,128,512]{2,1,0:T(8,128)(2,1)}, bf16[4,384,512]{2,1,0:T(8,128)(2,1...) custom-call(bf16[4,512,512]{2,1,0:T(8,128)(2,1)} %chars.3, s32[4,512]{1,0:T(4,128)} %lengths.3, ...), custom_call_target="tpu_custom_call" | custom-call | tf_op jit(solution)/shard_map/layer/pallas_call | solution.py:1091
  103.3 12.6 %spread.1 = (bf16[4,512,512]{2,1,0:T(8,128)(2,1)}, f32[4,512,512]{2,1,0:T(8,128)}, bf16[4,128,512]{2,1,0:T(8,128)(2,1)}, f32[512,512]{1,0:T(8,128)}, f32[512,512...) custom-call(s32[4,512]{1,0:T(4,128)} %lengths.3, ...), custom_call_target="tpu_custom_call" | custom-call | tf_op jit(solution)/shard_map/spread/pallas_call | solution.py:1125
